TPU v7x, 512 devices: a whole 4x4x16 slice. The times are simulated.
512 devices in a mesh: tr: 16 (over z), sec: 32 (over y, x, core).
Axes of the slice: x: 4, y: 4, z: 16, core: 2. Of those that a mesh axis runs over, the one named last changes fastest.
Arguments:
- psi: bfloat16 [32, 512, 8, 512], P('sec', 'tr'), may hold values from -24 to 24
- precond: bfloat16 [32, 512, 8, 512], P('sec', 'tr'), may hold values from 0.25 to 6
- env_left: bfloat16 [3, 32, 512, 512], P(None, 'sec'), may hold values from -1 to 2
- env_right: bfloat16 [3, 32, 512, 512], P(None, 'sec'), may hold values from -1 to 2
- mixers: bfloat16 [3, 8, 8], replicated, may hold values from -3 to 3
- sizes: int32 [32, 2], P('sec'), may hold values from 128 to 512, as said below
Outputs:
- psi_new: bfloat16 [32, 512, 8, 512], P('sec', 'tr')
- residual_new: bfloat16 [32, 512, 8, 512], P('sec', 'tr')
- energy: float32 [], replicated
Inputs may be any that keep to these rules, and one draw needn't show every extreme that they name: `sizes`: every entry is a multiple of 128; in each column some sector has 512.
All inputs are finite; a program needn't handle non-finite values.
Results may differ from a plain program's by a relative error of at most 0.023.
Values may be sent and summed in bfloat16 or wider, within the bound.
A program may use at most 64 MiB of HBM per device.

v0:
```python
import jax
import jax.numpy as jnp
from jax import lax
from jax.sharding import PartitionSpec as P

EPSILON = 1e-06


def shifted(block, axis, distance):
    devices = range(lax.axis_size(axis))
    route = [(i - distance, i) for i in devices if i - distance in devices]
    return lax.ppermute(block, axis, route)


def hamiltonian(basis, env_left, env_right, mixers, right_mask):
    lower = shifted(basis, "sec", 1)
    upper = shifted(basis, "sec", -1)
    sources = (basis, lower, upper)
    rows = basis.shape[1]
    phys = basis.shape[2]
    width = basis.shape[3]
    total = jnp.zeros((width, phys * rows), jnp.float32)
    for channel in range(3):
        mixed = jnp.einsum(
            "sbqa,pq->sbpa", sources[channel], mixers[channel], preferred_element_type=jnp.float32
        ).astype(jnp.bfloat16)
        half = jnp.einsum(
            "xc,ac->xa",
            mixed.reshape(rows * phys, width),
            env_left[channel, 0],
            preferred_element_type=jnp.float32,
        ).astype(jnp.bfloat16)
        swapped = lax.all_to_all(
            half.reshape(1, rows, phys, width), "tr", split_axis=3, concat_axis=1, tiled=True
        )
        total = total + jnp.dot(
            env_right[channel, 0],
            swapped.reshape(width, phys * rows),
            preferred_element_type=jnp.float32,
        )
    return total.reshape(1, width, phys, rows) * right_mask


def body(psi, precond, env_left, env_right, mixers, sizes):
    rows = psi.shape[1]
    phys = psi.shape[2]
    width = psi.shape[3]
    count = float(lax.axis_size("sec") * psi.shape[0] * width * phys * width)
    offset = lax.axis_index("tr") * rows
    local_rows = offset + jnp.arange(rows, dtype=jnp.int32)
    all_states = jnp.arange(width, dtype=jnp.int32)
    left_mask = ((local_rows < sizes[0, 1])[:, None] & (all_states < sizes[0, 0])[None, :]).astype(
        jnp.float32
    )
    left_mask = left_mask.reshape(1, rows, 1, width)
    right_mask = ((all_states < sizes[0, 1])[:, None] & (local_rows < sizes[0, 0])[None, :]).astype(
        jnp.float32
    )
    right_mask = right_mask.reshape(1, width, 1, rows)
    start = (psi * left_mask.astype(jnp.bfloat16)).astype(jnp.float32)
    start_sq = lax.psum(jnp.sum(start * start), ("tr", "sec"))
    basis0 = (start * lax.rsqrt(start_sq / count + EPSILON)).astype(jnp.bfloat16)
    first_vec = basis0.astype(jnp.float32)
    image0 = lax.all_to_all(
        hamiltonian(basis0, env_left, env_right, mixers, right_mask).astype(jnp.bfloat16),
        "tr",
        split_axis=1,
        concat_axis=3,
        tiled=True,
    ).astype(jnp.float32)
    factors = precond.astype(jnp.float32)
    theta = lax.psum(jnp.sum(first_vec * image0), ("tr", "sec")) / count
    trial = (image0 - theta * first_vec) * factors
    along = lax.psum(jnp.sum(first_vec * trial), ("tr", "sec")) / count
    trial = trial - along * first_vec
    fresh = lax.psum(jnp.sum(trial * trial), ("tr", "sec")) / count
    basis1 = (trial * lax.rsqrt(fresh + EPSILON)).astype(jnp.bfloat16)
    second_vec = basis1.astype(jnp.float32)
    image1 = lax.all_to_all(
        hamiltonian(basis1, env_left, env_right, mixers, right_mask).astype(jnp.bfloat16),
        "tr",
        split_axis=1,
        concat_axis=3,
        tiled=True,
    ).astype(jnp.float32)
    parts = lax.psum(
        (jnp.sum(first_vec * image1), jnp.sum(second_vec * image0), jnp.sum(second_vec * image1)),
        ("tr", "sec"),
    )
    cross = 0.5 * (parts[0] + parts[1]) / count
    corner = parts[2] / count
    halfgap = 0.5 * (theta - corner)
    energy = 0.5 * (theta + corner) - jnp.sqrt(halfgap * halfgap + cross * cross)
    weight_one = corner - energy
    weight_two = -cross
    scale = lax.rsqrt(weight_one * weight_one + weight_two * weight_two)
    ritz = (weight_one * first_vec + weight_two * second_vec) * scale
    ritz_image = (weight_one * image0 + weight_two * image1) * scale
    psi_new = ritz.astype(jnp.bfloat16)
    residual_new = (ritz_image - energy * ritz).astype(jnp.bfloat16)
    return (psi_new, residual_new, energy)


def solution(mesh):
    placed = (
        P("sec", "tr", None, None),
        P("sec", "tr", None, None),
        P(None, "sec", None, None),
        P(None, "sec", None, None),
        P(),
        P("sec", None),
    )
    return jax.shard_map(
        body,
        mesh=mesh,
        in_specs=placed,
        out_specs=(P("sec", "tr", None, None), P("sec", "tr", None, None), P()),
        check_vma=False,
    )
```

profile of v0, /device:TPU:1, one launch (start us, length us, event | category | flops | bytes accessed | tf_op | source)
XLA Modules:
  0.0 776.4 jit_solution(17750186646935784879)
XLA Ops:
  4.0 1.7 fusion.12
  5.7 111.0 %psum.49 = f32[]{:T(128)} all-reduce(f32[]{:T(128)} %fusion.12), channel_id=1, replica_groups=mesh['tr'=16,'sec'=32] {'tr','sec'}, use_global_device_ids=true, to_apply=%region_1.0 | all-reduce | flops 1 | bytes 8 | tf_op jit(solution)/shard_map/psum | solution.py:61
  120.8 1.7 reshape.303
  122.5 7.2 all-to-all-start
  129.7 2.1 collective-permute-start
  131.8 3.3 collective-permute-done
  137.4 1.7 reshape.305
  139.1 3.6 all-to-all-done
  142.7 11.0 %all-to-all-start.1 = ((bf16[16,2,4096]{2,1,0:T(2,128)(2,1)}), bf16[16,2,4096]{2,1,0:T(2,128)(2,1)S(1)}, u32[]{:S(2)}, u32[]{:S(2)}) async-start(bf16[16,2,4096]{2,1,0:T(2,128)(2,1)} %reshape.305), calls=%async_computation.1 | async-start | bytes 524288 | tf_op jit(solution)/shard_map/all_to_all | solution.py:33
  153.8 2.9 collective-permute-start.1
  156.7 5.0 collective-permute-done.1
  164.1 1.7 reshape.307
  166.8 11.6 %all-to-all-start.2 = ((bf16[16,2,4096]{2,1,0:T(2,128)(2,1)}), bf16[16,2,4096]{2,1,0:T(2,128)(2,1)}, u32[]{:S(2)}, u32[]{:S(2)}) async-start(bf16[16,2,4096]{2,1,0:T(2,128)(2,1)} %reshape.307), calls=%async_computation.2 | async-start | bytes 524288 | tf_op jit(solution)/shard_map/all_to_all | solution.py:33
  179.7 2.7 copy.87
  182.4 1.6 copy.67
  186.4 2.7 copy.88
  189.2 1.5 copy.70
  191.5 2.0 reshape.308
  193.5 2.7 copy.89
  202.8 24.2 %all_to_all.108 = bf16[16,2,4096]{2,1,0:T(2,128)(2,1)S(1)} all-to-all(bf16[16,2,4096]{2,1,0:T(2,128)(2,1)S(1)} %reshape.309), channel_id=1, replica_groups=mesh['tr'=16,'sec'=32] {'tr'}, dimensions={0} | all-to-all | bytes 524288 | tf_op jit(solution)/shard_map/all_to_all | solution.py:64
  228.5 2.4 copy.96
  232.6 108.2 %psum.50 = f32[]{:T(128)} all-reduce(f32[]{:T(128)} %fusion.18), channel_id=1, replica_groups=mesh['tr'=16,'sec'=32] {'tr','sec'}, use_global_device_ids=true, to_apply=%region_3.0 | all-reduce | flops 1 | bytes 8 | tf_op jit(solution)/shard_map/psum | solution.py:72
  342.2 99.4 %psum.51 = f32[]{:T(128)} all-reduce(f32[]{:T(128)} %fusion.21), channel_id=1, replica_groups=mesh['tr'=16,'sec'=32] {'tr','sec'}, use_global_device_ids=true, to_apply=%region_5.0 | all-reduce | flops 1 | bytes 8 | tf_op jit(solution)/shard_map/psum | solution.py:74
  443.0 100.3 %psum.52 = f32[]{:T(128)} all-reduce(f32[]{:T(128)} %multiply_reduce_fusion), channel_id=1, replica_groups=mesh['tr'=16,'sec'=32] {'tr','sec'}, use_global_device_ids=true, to_apply=%region_7.0 | all-reduce | flops 1 | bytes 8 | tf_op jit(solution)/shard_map/psum | solution.py:76
  544.2 1.6 fusion.3
  546.7 1.7 reshape.311
  548.4 5.4 all-to-all-start.4
  553.8 3.3 collective-permute-start.2
  557.1 3.3 collective-permute-done.2
  562.7 1.7 reshape.313
  564.4 2.5 all-to-all-done.4
  566.9 10.9 %all-to-all-start.5 = ((bf16[16,2,4096]{2,1,0:T(2,128)(2,1)}), bf16[16,2,4096]{2,1,0:T(2,128)(2,1)S(1)}, u32[]{:S(2)}, u32[]{:S(2)}) async-start(bf16[16,2,4096]{2,1,0:T(2,128)(2,1)} %reshape.313), calls=%async_computation.5 | async-start | bytes 524288 | tf_op jit(solution)/shard_map/all_to_all | solution.py:33
  577.9 2.9 collective-permute-start.3
  580.8 5.0 collective-permute-done.3
  588.2 1.7 reshape.315
  590.9 11.3 %all-to-all-start.6 = ((bf16[16,2,4096]{2,1,0:T(2,128)(2,1)}), bf16[16,2,4096]{2,1,0:T(2,128)(2,1)}, u32[]{:S(2)}, u32[]{:S(2)}) async-start(bf16[16,2,4096]{2,1,0:T(2,128)(2,1)} %reshape.315), calls=%async_computation.6 | async-start | bytes 524288 | tf_op jit(solution)/shard_map/all_to_all | solution.py:33
  602.8 2.7 copy.90
  605.5 1.6 copy.78
  608.5 2.1 fusion.32
  610.7 2.0 reshape.314
  612.6 2.7 copy.91
  618.3 2.0 reshape.316
  620.3 2.7 copy.92
  625.9 1.5 convolution_add_fusion.1
  629.6 24.4 %all_to_all.109 = bf16[16,2,4096]{2,1,0:T(2,128)(2,1)S(1)} all-to-all(bf16[16,2,4096]{2,1,0:T(2,128)(2,1)S(1)} %reshape.317), channel_id=1, replica_groups=mesh['tr'=16,'sec'=32] {'tr'}, dimensions={0} | all-to-all | bytes 524288 | tf_op jit(solution)/shard_map/all_to_all | solution.py:79
  655.5 2.4 copy.95
  658.8 1.8 fusion.23
  661.9 109.4 %all-reduce = (f32[]{:T(128)}, f32[]{:T(128)}) all-reduce(f32[]{:T(128)} %get-tuple-element.4, f32[]{:T(128)S(6)} %add.91), channel_id=1, replica_groups=mesh['tr'=16,'sec'=32] {'tr','sec'}, use_global_device_ids=true, to_apply=%region_9.0 | all-reduce | flops 2 | bytes 16 | tf_op jit(solution)/shard_map/psum | solution.py:86
  (73 shorter events, 48.2 us)
Async XLA Ops:
  119.9 15.2 %copy-start.9 = (bf16[3,8,8]{2,1,0:T(8,128)(2,1)S(1)}, bf16[3,8,8]{2,1,0:T(8,128)(2,1)}, u32[]{:S(2)}) copy-start(bf16[3,8,8]{2,1,0:T(8,128)(2,1)} %param.10) | copy-start | bytes 1156
  122.5 20.2 %all-to-all-start = ((bf16[16,2,4096]{2,1,0:T(2,128)(2,1)}), bf16[16,2,4096]{2,1,0:T(2,128)(2,1)S(1)}, u32[]{:S(2)}, u32[]{:S(2)}) async-start(bf16[16,2,4096]{2,1,0:T(2,128)(2,1)} %reshape.303), calls=%async_computation | async-start | bytes 524288 | tf_op jit(solution)/shard_map/all_to_all | solution.py:33
  129.7 5.4 collective-permute-start
  142.7 24.1 %all-to-all-start.1 = ((bf16[16,2,4096]{2,1,0:T(2,128)(2,1)}), bf16[16,2,4096]{2,1,0:T(2,128)(2,1)S(1)}, u32[]{:S(2)}, u32[]{:S(2)}) async-start(bf16[16,2,4096]{2,1,0:T(2,128)(2,1)} %reshape.305), calls=%async_computation.1 | async-start | bytes 524288 | tf_op jit(solution)/shard_map/all_to_all | solution.py:33
  153.8 8.0 %collective-permute-start.1 = (bf16[1,32,8,512]{3,2,1,0:T(8,128)(2,1)S(1)}, bf16[1,32,8,512]{3,2,1,0:T(8,128)(2,1)S(1)}, u32[]{:S(2)}, u32[]{:S(2)}) collective-permute-start(bf16[1,32,8,512]{3,2,1,0:T(8,128)(2,1)S(1)} %fusion.13), channel_id=1, source_target_pairs={{1,0},{2,1},{3,2},{4,3},{5,4},{6,5},{7,6},{8,7},{9,8},{10,9},{11,1... | collective-permute-start | bytes 786440 | tf_op jit(solution)/shard_map/ppermute | solution.py:12
  166.8 24.7 %all-to-all-start.2 = ((bf16[16,2,4096]{2,1,0:T(2,128)(2,1)}), bf16[16,2,4096]{2,1,0:T(2,128)(2,1)}, u32[]{:S(2)}, u32[]{:S(2)}) async-start(bf16[16,2,4096]{2,1,0:T(2,128)(2,1)} %reshape.307), calls=%async_computation.2 | async-start | bytes 524288 | tf_op jit(solution)/shard_map/all_to_all | solution.py:33
  182.4 2.3 copy-start.1
  199.2 1.4 copy-start.6
  230.9 1.0 copy-start
  230.9 110.5 %copy-start.3 = (bf16[1,32,8,512]{3,2,1,0:T(8,128)(2,1)S(1)}, bf16[1,32,8,512]{3,2,1,0:T(8,128)(2,1)}, u32[]{:S(2)}) copy-start(bf16[1,32,8,512]{3,2,1,0:T(8,128)(2,1)} %param.7) | copy-start | bytes 786436
  544.2 33.6 %copy-start.4 = (bf16[1,32,8,512]{3,2,1,0:T(8,128)(2,1)}, bf16[1,32,8,512]{3,2,1,0:T(8,128)(2,1)S(1)}, u32[]{:S(2)}) copy-start(bf16[1,32,8,512]{3,2,1,0:T(8,128)(2,1)S(1)} %multiply_convert_fusion.1) | copy-start | bytes 786436
  548.4 18.6 %all-to-all-start.4 = ((bf16[16,2,4096]{2,1,0:T(2,128)(2,1)}), bf16[16,2,4096]{2,1,0:T(2,128)(2,1)S(1)}, u32[]{:S(2)}, u32[]{:S(2)}) async-start(bf16[16,2,4096]{2,1,0:T(2,128)(2,1)} %reshape.311), calls=%async_computation.4 | async-start | bytes 524288 | tf_op jit(solution)/shard_map/all_to_all | solution.py:33
  553.8 6.6 collective-permute-start.2
  566.9 24.0 %all-to-all-start.5 = ((bf16[16,2,4096]{2,1,0:T(2,128)(2,1)}), bf16[16,2,4096]{2,1,0:T(2,128)(2,1)S(1)}, u32[]{:S(2)}, u32[]{:S(2)}) async-start(bf16[16,2,4096]{2,1,0:T(2,128)(2,1)} %reshape.313), calls=%async_computation.5 | async-start | bytes 524288 | tf_op jit(solution)/shard_map/all_to_all | solution.py:33
  577.9 8.0 %collective-permute-start.3 = (bf16[1,32,8,512]{3,2,1,0:T(8,128)(2,1)S(1)}, bf16[1,32,8,512]{3,2,1,0:T(8,128)(2,1)S(1)}, u32[]{:S(2)}, u32[]{:S(2)}) collective-permute-start(bf16[1,32,8,512]{3,2,1,0:T(8,128)(2,1)S(1)} %multiply_convert_fusion.1), channel_id=1, source_target_pairs={{1,0},{2,1},{3,2},{4,3},{5,4},{6,5},{7,6},{8,7},{9,8},{10,9},{11,1... | collective-permute-start | bytes 786440 | tf_op jit(solution)/shard_map/ppermute | solution.py:12
  590.9 14.6 %copy-start.8 = (bf16[16,2,4096]{2,1,0:T(2,128)(2,1)}, bf16[16,2,4096]{2,1,0:T(2,128)(2,1)S(1)}, u32[]{:S(2)}) copy-start(bf16[16,2,4096]{2,1,0:T(2,128)(2,1)S(1)} %all-to-all-done.5) | copy-start | bytes 786436
  590.9 27.4 %all-to-all-start.6 = ((bf16[16,2,4096]{2,1,0:T(2,128)(2,1)}), bf16[16,2,4096]{2,1,0:T(2,128)(2,1)}, u32[]{:S(2)}, u32[]{:S(2)}) async-start(bf16[16,2,4096]{2,1,0:T(2,128)(2,1)} %reshape.315), calls=%async_computation.6 | async-start | bytes 524288 | tf_op jit(solution)/shard_map/all_to_all | solution.py:33
  605.5 3.1 copy-start.2
  625.9 1.5 copy-start.7
  658.8 115.2 %copy-start.5 = (bf16[1,32,8,512]{3,2,1,0:T(8,128)(2,1)S(1)}, bf16[1,32,8,512]{3,2,1,0:T(8,128)(2,1)}, u32[]{:S(2)}) copy-start(bf16[1,32,8,512]{3,2,1,0:T(8,128)(2,1)} %copy-done.4) | copy-start | bytes 786436
where the time goes:
time: 785 us; the launch traced here: 776 us
  blocking collectives  577 us (74%)
  local copies, waits for them, and re-layouts  69.8 us (9%)
  starting transfers between devices  68.8 us (9%)
  waiting for transfers between devices  25 us (3%)
  matrix products  15.9 us (2%)
  other arithmetic  11 us (1%)
  between operations  9.17 us (1%)
    psum x1, blocking collectives, body(): start_sq = lax.psum(jnp.sum(start * start), ('tr', 'sec'))  111 us
    psum x1, blocking collectives, body(): lax.psum((jnp.sum(first_vec * image1), jnp.sum(second_vec * image0), jnp....  109 us
    psum x1, blocking collectives, body(): theta = lax.psum(jnp.sum(first_vec * image0), ('tr', 'sec')) / count  108 us
    psum x1, blocking collectives, body(): fresh = lax.psum(jnp.sum(trial * trial), ('tr', 'sec')) / count  100 us
    psum x1, blocking collectives, body(): along = lax.psum(jnp.sum(first_vec * trial), ('tr', 'sec')) / count  99.4 us
    all_to_all x6, starting transfers between devices, hamiltonian(): lax.all_to_all(half.reshape(1, rows, phys, width), 'tr', split_axis=3, co...  57.5 us
    all_to_all x12, local copies, waits for them, and re-layouts, hamiltonian(): lax.all_to_all(half.reshape(1, rows, phys, width), 'tr', split_axis=3, co...  25.6 us
    all_to_all x1, blocking collectives, body(): lax.all_to_all(hamiltonian(basis1, env_left, env_right, mixers, right_mas...  24.4 us
  transfers between devices with their start and end apart: 10, of which 9 were waited for; matrix products, arithmetic and copies ran while one was open for 6% of the time, Pallas kernels for 0%

commit v1 on v0

v1 whole, which is shorter than its diff:
```python
import jax
import jax.numpy as jnp
from jax import lax
from jax.experimental import pallas as pl
from jax.experimental.pallas import tpu as pltpu
from jax.sharding import PartitionSpec as P

EPSILON = 1e-06
MESH = pl.DeviceIdType.MESH
F32 = jnp.float32
BF16 = jnp.bfloat16
TR = 16
SEC = 32
ROWS = 32
PHYS = 8
WIDTH = 512
HALF = 256
LINES = ROWS * PHYS
COUNT = float(SEC * WIDTH * PHYS * WIDTH)
STEPS = (1, 3, 2)


def dot(a, b):
    return jnp.dot(a, b, preferred_element_type=F32)


def dot_nt(a, b):
    return lax.dot_general(a, b, (((1,), (1,)), ((), ())), preferred_element_type=F32)


def iota(shape, axis):
    return lax.broadcasted_iota(jnp.int32, shape, axis)


def partial_sum(x):
    rows = jnp.sum(x, axis=0, keepdims=True)
    total = rows[:, 0:128]
    for lane in range(128, x.shape[1], 128):
        total = total + rows[:, lane : lane + 128]
    return total


def phys_major(block):
    pieces = [jnp.concatenate([block[2 * p], block[2 * p + 1]], axis=1) for p in range(PHYS)]
    return jnp.concatenate(pieces, axis=0)


def columns_of(value):
    blocks = []
    for j in range(TR):
        p, side = divmod(j, 2)
        blocks.append(value[p * ROWS : (p + 1) * ROWS, side * HALF : (side + 1) * HALF])
    return jnp.stack(blocks, axis=0)


def kernel(
    psi_hbm,
    pc_hbm,
    left_hbm,
    right_hbm,
    mix_hbm,
    sizes_hbm,
    psi_out,
    res_out,
    energy_out,
    psi_in,
    pc_in,
    mix,
    sizes,
    own_env,
    land_env,
    env,
    kron,
    to_new,
    to_old,
    start_rows,
    cols_send,
    cols_mid,
    cols,
    near_cols,
    turn_send,
    turn_recv,
    pc_send,
    pc_mid,
    pc_new,
    vec,
    near_vec,
    half_send,
    half_recv,
    first_send,
    first_mid,
    first_old,
    second_send,
    second_mid,
    second_old,
    red_send,
    red_tr,
    red_sec,
    in_sem,
    scatter_send_sem,
    scatter_recv_sem,
    own_send_sem,
    own_recv_sem,
    gather_send_sem,
    gather_recv_sem,
    near_send_sem,
    near_recv_sem,
    turn_send_sem,
    turn_recv_sem,
    move_send_sem,
    move_one_sem,
    move_two_sem,
    red_send_sem,
    red_recv_sem,
):
    z = lax.axis_index("tr")
    sec = lax.axis_index("sec")
    k = sec // 2
    core = lax.rem(sec, 2)
    y = k // 4
    x = lax.rem(k, 4)

    def ring(z2):
        return {"tr": z2}

    def plane(k2):
        return {"sec": 2 * k2 + core}

    def turned(m):
        return jnp.where(m >= TR - 1, m - (TR - 1), m)

    def ring_peer(i):
        m = turned(i + k)
        step = m // 2 + 1
        return lax.rem(z + jnp.where(lax.rem(m, 2) == 0, step, TR - step), TR)

    def ring_source(i):
        m = turned(i + k)
        step = m // 2 + 1
        return lax.rem(z + jnp.where(lax.rem(m, 2) == 0, TR - step, step), TR)

    def plane_peer(i):
        return 4 * lax.rem(y + i // 4, 4) + lax.rem(x + lax.rem(i, 4), 4)

    def remote(src, dst, send_sem, recv_sem, device):
        return pltpu.make_async_remote_copy(
            src_ref=src,
            dst_ref=dst,
            send_sem=send_sem,
            recv_sem=recv_sem,
            device_id=device,
            device_id_type=MESH,
        )

    def several(ref, count, send_sem, recv_sem):
        part = ref.at[pl.ds(0, count)]
        return remote(part, part, send_sem, recv_sem, ring(lax.rem(z + 1, TR)))

    ends = []

    loads = [
        pltpu.make_async_copy(psi_hbm.at[0], psi_in, in_sem.at[0]),
        pltpu.make_async_copy(pc_hbm.at[0], pc_in, in_sem.at[1]),
        pltpu.make_async_copy(mix_hbm, mix, in_sem.at[2]),
        pltpu.make_async_copy(sizes_hbm, sizes, in_sem.at[3]),
    ]
    env_loads = [
        pltpu.make_async_copy(right_hbm.at[:, 0], own_env.at[0], in_sem.at[4]),
        pltpu.make_async_copy(left_hbm.at[:, 0], own_env.at[1], in_sem.at[5]),
    ]
    for load in loads:
        load.start()
    gap = lax.rem(z - k + TR + 1, TR)

    @pl.when(gap < 3)
    def _():
        for load in env_loads:
            load.start()

    barrier = pltpu.get_barrier_semaphore()

    def greet_tr(i, carry):
        pl.semaphore_signal(barrier, inc=1, device_id=ring(lax.rem(z + i, TR)), device_id_type=MESH)
        return carry

    def greet_sec(i, carry):
        pl.semaphore_signal(
            barrier, inc=1, device_id={"sec": lax.rem(sec + i, SEC)}, device_id_type=MESH
        )
        return carry

    partner = sec + 1 - 2 * core
    pl.semaphore_signal(
        barrier,
        inc=1,
        device_id={"tr": lax.rem(z + 2 * core - 1 + TR, TR), "sec": partner},
        device_id_type=MESH,
    )
    lax.fori_loop(1, SEC, greet_sec, 0)
    lax.fori_loop(1, TR, greet_tr, 0)

    line = iota((LINES, LINES), 0)
    other = iota((LINES, LINES), 1)

    def to_phys_major(value):
        matrix = ((line // ROWS) == lax.rem(other, PHYS)) & (
            lax.rem(line, ROWS) == (other // PHYS)
        )
        return dot(matrix.astype(BF16), value)

    def to_row_major(value):
        matrix = ((other // ROWS) == lax.rem(line, PHYS)) & (
            lax.rem(other, ROWS) == (line // PHYS)
        )
        return dot(matrix.astype(BF16), value)

    loads[3].wait()
    used_left = sizes[0, 0]
    used_right = sizes[0, 1]
    keep = ((z * ROWS + iota((LINES, WIDTH), 0) // PHYS) < used_right) & (
        iota((LINES, WIDTH), 1) < used_left
    )
    loads[0].wait()
    start = jnp.where(keep, psi_in[...].astype(F32).reshape(LINES, WIDTH), 0.0).astype(BF16)
    start_rows[...] = start
    cols_send[...] = columns_of(to_phys_major(start).astype(BF16))
    loads[1].wait()
    pc_send[...] = pc_in[...].astype(F32).reshape(TR, 2 * PHYS, WIDTH).astype(BF16)

    pl.semaphore_wait(barrier, TR + SEC - 1)

    def move_in_plane(n, source, middle):
        def send(i, carry):
            peer = plane_peer(i)
            remote(
                source.at[peer],
                middle.at[k],
                move_send_sem.at[n, 0],
                move_one_sem.at[n, k],
                plane(peer),
            ).start()
            return carry

        lax.fori_loop(1, TR, send, 0)
        middle[k] = source[k]
        ends.append(several(middle, TR - 1, move_send_sem.at[n, 0], move_two_sem.at[n]))

    def arrived(n, middle, index):
        return remote(
            middle.at[index],
            middle.at[index],
            move_send_sem.at[n, 0],
            move_one_sem.at[n, index],
            ring(lax.rem(z + 1, TR)),
        )

    def move_in_ring(n, middle, target):
        def send(i, carry):
            peer = ring_peer(i)

            @pl.when(peer != k)
            def _():
                arrived(n, middle, peer).wait_recv()

            remote(
                middle.at[peer], target.at[z], move_send_sem.at[n, 1], move_two_sem.at[n], ring(peer)
            ).start()
            return carry

        lax.fori_loop(0, TR - 1, send, 0)

        @pl.when(z != k)
        def _():
            arrived(n, middle, z).wait_recv()

        target[z] = middle[z]
        done = several(target, TR - 1, move_send_sem.at[n, 1], move_two_sem.at[n])
        ends.append(done)
        return done

    def back_in_ring(n, source, middle):
        def send(i, carry):
            peer = ring_peer(i)
            remote(
                source.at[peer],
                middle.at[z],
                move_send_sem.at[n, 0],
                move_one_sem.at[n, z],
                ring(peer),
            ).start()
            return carry

        lax.fori_loop(0, TR - 1, send, 0)
        middle[z] = source[z]
        ends.append(several(middle, TR - 1, move_send_sem.at[n, 0], move_two_sem.at[n]))

    def back_in_plane(n, middle, target):
        def forward(index):
            @pl.when(index != k)
            def _():
                remote(
                    middle.at[index],
                    target.at[k],
                    move_send_sem.at[n, 1],
                    move_two_sem.at[n],
                    plane(index),
                ).start()

        def send(i, carry):
            index = ring_source(i)
            arrived(n, middle, index).wait_recv()
            forward(index)
            return carry

        forward(z)
        lax.fori_loop(0, TR - 1, send, 0)
        target[k] = middle[k]
        done = several(target, TR - 1, move_send_sem.at[n, 1], move_two_sem.at[n])
        ends.append(done)
        return done

    def piece(m, i, rows=ROWS, first=0):
        return env.at[m, :, pl.ds(pl.multiple_of(i * ROWS + first, 16), rows), :]

    def scatter(m):
        used = used_right if m == 0 else used_left
        for d in range(3):

            @pl.when(gap == d)
            def _():
                env_loads[m].wait()
                for i in range(d, TR, 3):
                    span = pl.ds(i * ROWS, ROWS)
                    rows = own_env[m, :, span, :]
                    own_env[m, :, span, :] = jnp.where(i * ROWS < used, rows, jnp.zeros_like(rows))

                    @pl.when(k != i)
                    def _():
                        remote(
                            own_env.at[m, :, span, :],
                            land_env.at[m],
                            scatter_send_sem.at[m, i],
                            scatter_recv_sem.at[m],
                            plane(i),
                        ).start()

                    @pl.when(k == i)
                    def _():
                        land_env[m] = own_env[m, :, span, :]

    def scatter_end(m):
        for d in range(3):

            @pl.when(gap == d)
            def _():
                for i in range(d, TR, 3):

                    @pl.when(k != i)
                    def _():
                        remote(
                            own_env.at[m, :, pl.ds(i * ROWS, ROWS), :],
                            land_env.at[m],
                            scatter_send_sem.at[m, i],
                            scatter_recv_sem.at[m],
                            plane(i),
                        ).wait_send()

    shift = lax.rem(k, 3) - 1
    home = lax.rem(z - shift + TR, TR)

    def hand_over(m):
        return remote(
            land_env.at[m], piece(m, k), own_send_sem.at[m], own_recv_sem.at[m], ring(home)
        )

    def keep_here(m):
        return pltpu.make_async_copy(land_env.at[m], piece(m, k), own_recv_sem.at[m])

    def own_start(m):
        @pl.when(home != k)
        def _():
            remote(
                land_env.at[m],
                land_env.at[m],
                own_send_sem.at[m],
                scatter_recv_sem.at[m],
                ring(lax.rem(z + 1, TR)),
            ).wait_recv()

        @pl.when(shift != 0)
        def _():
            hand_over(m).start()

        @pl.when(shift == 0)
        def _():
            keep_here(m).start()

    def own_wait(m):
        @pl.when(shift != 0)
        def _():
            hand_over(m).wait_recv()

        @pl.when(shift == 0)
        def _():
            keep_here(m).wait()

    def row_peer(step):
        return 4 * y + lax.rem(x + step, 4)

    def column_peer(step):
        return 4 * lax.rem(y + step, 4) + x

    def gather_copy(m, ref, i, side, target):
        return remote(ref, ref, gather_send_sem.at[m], gather_recv_sem.at[m, i, side], plane(target))

    def gather_direct(m):
        for step in STEPS:
            gather_copy(m, piece(m, k), k, 0, row_peer(step)).start()
            gather_copy(m, piece(m, k), k, 0, column_peer(step)).start()

    def gather_forward(m):
        for step in STEPS:
            source = row_peer(4 - step)
            gather_copy(m, piece(m, source), source, 0, source).wait_recv()
            for turn in STEPS:
                gather_copy(m, piece(m, source, 16, 0), source, 0, column_peer(turn)).start()
            source = column_peer(4 - step)
            gather_copy(m, piece(m, source), source, 0, source).wait_recv()
            for turn in STEPS:
                gather_copy(m, piece(m, source, 16, 16), source, 1, row_peer(turn)).start()

    def gather_wait(m):
        for dy in STEPS:
            for dx in STEPS:
                source = 4 * lax.rem(y + dy, 4) + lax.rem(x + dx, 4)
                gather_copy(m, piece(m, source, 16, 0), source, 0, source).wait_recv()
                gather_copy(m, piece(m, source, 16, 16), source, 1, source).wait_recv()

    def gather_end(m):
        sent = env.at[m, :, pl.ds(0, WIDTH - ROWS), :]
        remote(
            sent, sent, gather_send_sem.at[m], own_recv_sem.at[m], ring(lax.rem(z + 1, TR))
        ).wait_send()

    def turn(n, source, target):
        def send(i, carry):
            peer = plane_peer(i)
            remote(
                source.at[peer], target.at[k], turn_send_sem.at[n], turn_recv_sem.at[n], plane(peer)
            ).start()
            return carry

        lax.fori_loop(1, TR, send, 0)
        target[k] = source[k]
        done = several(target, TR - 1, turn_send_sem.at[n], turn_recv_sem.at[n])
        ends.append(done)
        return done

    sector = 2 * z + core

    def shifts(n, source, target):
        copies = []
        for way in range(2):
            copy = remote(
                source,
                target.at[way],
                near_send_sem.at[n, way],
                near_recv_sem.at[n, way],
                {"tr": lax.rem(z + core - way + TR, TR), "sec": partner},
            )
            copy.start()
            copies.append(copy)
        ends.extend(copies)
        return copies

    def inside(way, value):
        exists = sector > 0 if way == 0 else sector < SEC - 1
        return jnp.where(exists, value, jnp.zeros_like(value))

    move_in_plane(0, cols_send, cols_mid)
    scatter(0)
    scatter(1)
    own_start(0)
    cols_done = move_in_ring(0, cols_mid, cols)
    own_start(1)
    own_wait(0)
    gather_direct(0)
    move_in_plane(1, pc_send, pc_mid)

    wide_line = iota((WIDTH, WIDTH), 0)
    wide_other = iota((WIDTH, WIDTH), 1)

    def old_row(r):
        return lax.rem(r, 32) // 2 * 32 + r // 32 * 2 + lax.rem(r, 2)

    to_new[...] = (old_row(wide_line) == wide_other).astype(BF16)
    gather_forward(0)
    own_wait(1)
    gather_direct(1)
    to_old[...] = (old_row(wide_other) == wide_line).astype(BF16)
    loads[2].wait()
    spread = ((iota((LINES, PHYS), 0) // ROWS) == iota((LINES, PHYS), 1)).astype(BF16)
    same_row = lax.rem(line, ROWS) == lax.rem(other, ROWS)
    for c in range(3):
        mixed = dot_nt(dot(spread, mix[c]).astype(BF16), spread)
        kron[c] = jnp.where(same_row, mixed, 0.0).astype(BF16)

    cols_done.wait_recv()
    copies = shifts(0, cols, near_cols)
    own_cols = cols[...].reshape(WIDTH, HALF)
    gather_wait(0)
    turns = []

    def reordered(value):
        return dot(to_new[...], value).astype(BF16).reshape(TR, ROWS, HALF)

    def right_part(c, value):
        return reordered(dot(env[0, c], value).astype(BF16))

    turn_send[0, :, 0] = right_part(0, own_cols)
    turn_send[0, :, 1] = reordered(own_cols)
    turns.append(turn(0, turn_send.at[0], turn_recv.at[0]))
    gather_forward(1)
    for way in range(2):
        copies[way].wait_recv()
        turn_send[1, :, way] = right_part(
            way + 1, inside(way, near_cols[way].reshape(WIDTH, HALF))
        )
    turns.append(turn(1, turn_send.at[1], turn_recv.at[1]))
    pc_done = move_in_ring(1, pc_mid, pc_new)
    gather_wait(1)
    total = None
    for c, (group, place) in enumerate(((0, 0), (1, 0), (1, 1))):
        if place == 0:
            turns[group].wait_recv()
        mixed = dot(kron[c], phys_major(turn_recv[group, :, place])).astype(BF16)
        term = dot_nt(mixed, env[1, c])
        total = term if total is None else total + term
    rounded = total.astype(BF16)
    first_send[...] = to_row_major(rounded).astype(BF16).reshape(TR, 2 * PHYS, WIDTH)
    image0 = rounded.astype(F32)
    s = phys_major(turn_recv[0, :, 1]).astype(F32)
    pc_done.wait_recv()
    factors = to_phys_major(pc_new[...].reshape(LINES, WIDTH))

    def tr_start(h, block):
        red_send[h, 0] = block

        def send(i, carry):
            remote(
                red_send.at[h, 0],
                red_tr.at[h, z],
                red_send_sem.at[h, 0],
                red_recv_sem.at[h, 0],
                ring(ring_peer(i)),
            ).start()
            return carry

        lax.fori_loop(0, TR - 1, send, 0)
        red_tr[h, z] = block
        done = several(red_tr.at[h], TR - 1, red_send_sem.at[h, 0], red_recv_sem.at[h, 0])
        ends.append(done)
        return done

    def sec_start(h, block):
        red_send[h, 1] = block

        def send(i, carry):
            remote(
                red_send.at[h, 1],
                red_sec.at[h, sec],
                red_send_sem.at[h, 1],
                red_recv_sem.at[h, 1],
                {"sec": lax.rem(sec + i, SEC)},
            ).start()
            return carry

        lax.fori_loop(1, SEC, send, 0)
        red_sec[h, sec] = block
        done = several(red_sec.at[h], SEC - 1, red_send_sem.at[h, 1], red_recv_sem.at[h, 1])
        ends.append(done)
        return done

    def means(block):
        whole = jnp.sum(block, axis=1, keepdims=True)
        return [whole[n : n + 1] / COUNT for n in range(4)]

    weighted = s * factors
    parts = (s * s, s * image0, weighted * image0, weighted * s)
    block = jnp.concatenate([partial_sum(part) for part in parts] * 2, axis=0)
    tr_start(0, block).wait_recv()
    back_in_ring(2, first_send, first_mid)
    sec_start(0, jnp.sum(red_tr[0], axis=0)).wait_recv()
    ss, sw, spw, sps = means(jnp.sum(red_sec[0], axis=0))
    norm = lax.rsqrt(ss + EPSILON)
    theta = norm * norm * sw
    along = norm * norm * (spw - theta * sps)

    def trial_of(image, vector, weights):
        return (image - theta * vector) * weights - along * vector

    trial = trial_of(image0, s, factors)
    trial_bf = trial.astype(BF16)
    vec[...] = trial_bf

    copies = shifts(1, vec, near_vec)
    turns = []

    def left_part(c, value):
        mixed = dot(kron[c], value).astype(BF16)
        return columns_of(dot_nt(mixed, env[1, c]).astype(BF16))

    half_send[0, :, 0] = left_part(0, trial_bf)
    half_send[0, :, 1] = columns_of(trial_bf)
    turns.append(turn(2, half_send.at[0], half_recv.at[0]))
    for way in range(2):
        copies[way].wait_recv()
        half_send[1, :, way] = left_part(way + 1, inside(way, near_vec[way]))
    turns.append(turn(3, half_send.at[1], half_recv.at[1]))
    second = trial_bf.astype(F32)
    tt = partial_sum(trial * trial)
    t0 = partial_sum(second * image0)
    total = None
    for c, (group, place) in enumerate(((0, 0), (1, 0), (1, 1))):
        if place == 0:
            turns[group].wait_recv()
        half = dot(to_old[...], half_recv[group, :, place].reshape(WIDTH, HALF)).astype(BF16)
        term = dot(env[0, c], half)
        total = term if total is None else total + term
    second_send[...] = total.astype(BF16).reshape(TR, ROWS, HALF)
    back_in_ring(3, second_send, second_mid)
    image1_cols = total.astype(BF16).astype(F32)
    trial_cols = dot(to_old[...], half_recv[0, :, 1].reshape(WIDTH, HALF))
    s1 = partial_sum(cols[...].reshape(WIDTH, HALF).astype(F32) * image1_cols)
    t1 = partial_sum(trial_cols * image1_cols)
    block = jnp.concatenate([tt, s1, t0, t1] * 2, axis=0)
    sec_start(1, block).wait_recv()
    sums_done = tr_start(1, jnp.sum(red_sec[1], axis=0))
    first_done = back_in_plane(2, first_mid, first_old)
    second_done = back_in_plane(3, second_mid, second_old)
    sums_done.wait_recv()
    tt, s1, t0, t1 = means(jnp.sum(red_tr[1], axis=0))

    fresh = norm * norm * tt
    grow = norm * lax.rsqrt(fresh + EPSILON)
    cross = 0.5 * norm * grow * (s1 + t0)
    corner = grow * grow * t1
    halfgap = 0.5 * (theta - corner)
    energy = 0.5 * (theta + corner) - jnp.sqrt(halfgap * halfgap + cross * cross)
    weight_one = corner - energy
    weight_two = -cross
    scale = lax.rsqrt(weight_one * weight_one + weight_two * weight_two)
    one = weight_one * scale * norm
    two = weight_two * scale * grow
    energy_out[...] = energy

    first_done.wait_recv()
    old_image = first_old[...].reshape(LINES, WIDTH).astype(F32)
    old_start = start_rows[...].astype(F32)
    old_factors = pc_send[...].reshape(LINES, WIDTH).astype(F32)
    old_trial = trial_of(old_image, old_start, old_factors).astype(BF16).astype(F32)
    ritz = one * old_start + two * old_trial
    psi_out[...] = ritz.reshape(ROWS, PHYS, WIDTH).astype(BF16)[None]
    partial = one * old_image - energy * ritz
    second_done.wait_recv()
    residual = partial + two * to_row_major(phys_major(second_old[...]))
    res_out[...] = residual.reshape(ROWS, PHYS, WIDTH).astype(BF16)[None]

    for m in range(2):
        scatter_end(m)
        gather_end(m)

        @pl.when(shift != 0)
        def _():
            hand_over(m).wait_send()

    for end in ends:
        end.wait_send()


def body(psi, precond, env_left, env_right, mixers, sizes):
    anywhere = pl.BlockSpec(memory_space=pl.ANY)
    vmem = pl.BlockSpec(memory_space=pltpu.VMEM)
    dma = pltpu.SemaphoreType.DMA
    columns = (TR, ROWS, HALF)
    pairs = (2, TR, 2, ROWS, HALF)
    rows = (TR, 2 * PHYS, WIDTH)
    psi_new, residual_new, energy = pl.pallas_call(
        kernel,
        out_shape=(
            jax.ShapeDtypeStruct(psi.shape, BF16),
            jax.ShapeDtypeStruct(psi.shape, BF16),
            jax.ShapeDtypeStruct((1, 1), F32),
        ),
        in_specs=[anywhere] * 6,
        out_specs=(vmem, vmem, vmem),
        scratch_shapes=[
            pltpu.VMEM((ROWS, PHYS, WIDTH), BF16),
            pltpu.VMEM((ROWS, PHYS, WIDTH), BF16),
            pltpu.VMEM((3, PHYS, PHYS), BF16),
            pltpu.SMEM((1, 2), jnp.int32),
            pltpu.VMEM((2, 3, WIDTH, WIDTH), BF16),
            pltpu.VMEM((2, 3, ROWS, WIDTH), BF16),
            pltpu.VMEM((2, 3, WIDTH, WIDTH), BF16),
            pltpu.VMEM((3, LINES, LINES), BF16),
            pltpu.VMEM((WIDTH, WIDTH), BF16),
            pltpu.VMEM((WIDTH, WIDTH), BF16),
            pltpu.VMEM((LINES, WIDTH), BF16),
            pltpu.VMEM(columns, BF16),
            pltpu.VMEM(columns, BF16),
            pltpu.VMEM(columns, BF16),
            pltpu.VMEM((2, *columns), BF16),
            pltpu.VMEM(pairs, BF16),
            pltpu.VMEM(pairs, BF16),
            pltpu.VMEM(rows, BF16),
            pltpu.VMEM(rows, BF16),
            pltpu.VMEM(rows, BF16),
            pltpu.VMEM((LINES, WIDTH), BF16),
            pltpu.VMEM((2, LINES, WIDTH), BF16),
            pltpu.VMEM(pairs, BF16),
            pltpu.VMEM(pairs, BF16),
            pltpu.VMEM(rows, BF16),
            pltpu.VMEM(rows, BF16),
            pltpu.VMEM(rows, BF16),
            pltpu.VMEM(columns, BF16),
            pltpu.VMEM(columns, BF16),
            pltpu.VMEM(columns, BF16),
            pltpu.VMEM((2, 2, 8, 128), F32),
            pltpu.VMEM((2, TR, 8, 128), F32),
            pltpu.VMEM((2, SEC, 8, 128), F32),
            dma((6,)),
            dma((2, TR)),
            dma((2,)),
            dma((2,)),
            dma((2,)),
            dma((2,)),
            dma((2, TR, 2)),
            dma((2, 2)),
            dma((2, 2)),
            dma((4,)),
            dma((4,)),
            dma((4, 2)),
            dma((4, TR)),
            dma((4,)),
            dma((2, 2)),
            dma((2, 2)),
        ],
        compiler_params=pltpu.CompilerParams(
            collective_id=0, has_side_effects=True, vmem_limit_bytes=60 * 1024 * 1024
        ),
        cost_estimate=pl.CostEstimate(
            flops=2_200_000_000, bytes_accessed=2_000_000, transcendentals=0
        ),
    )(psi, precond, env_left, env_right, mixers, sizes)
    return psi_new, residual_new, energy.reshape(())


def solution(mesh):
    placed = (
        P("sec", "tr", None, None),
        P("sec", "tr", None, None),
        P(None, "sec", None, None),
        P(None, "sec", None, None),
        P(),
        P("sec", None),
    )
    return jax.shard_map(
        body,
        mesh=mesh,
        in_specs=placed,
        out_specs=(P("sec", "tr", None, None), P("sec", "tr", None, None), P()),
        check_vma=False,
    )
```

time: 785 us -> 137 us (0.17)
  blocking collectives: 577 us -> 0 us
  Pallas kernels: 0 us -> 129 us
  starting transfers between devices: 68.8 us -> 0 us
  local copies, waits for them, and re-layouts: 69.8 us -> 3.34 us
  waiting for transfers between devices: 25 us -> 0 us
  matrix products: 15.9 us -> 0 us
  other arithmetic: 11 us -> 0 us
    psum x5 -> x0, blocking collectives: 528 us -> none  [the longest x1 111 us: body(): start_sq = lax.psum(jnp.sum(start * start), ('tr', 'sec'))]
    pallas_call x0 -> x1, Pallas kernels: none -> 129 us  [body(): pl.pallas_call(kernel, out_shape=(jax.ShapeDtypeStruct(psi.shape, BF16),...]
    all_to_all x6 -> x0, starting transfers between devices: 57.5 us -> none  [hamiltonian(): lax.all_to_all(half.reshape(1, rows, phys, width), 'tr', split_axis=3, co...]
    all_to_all x2 -> x0, blocking collectives: 48.5 us -> none  [the longest x1 24.4 us: body(): lax.all_to_all(hamiltonian(basis1, env_left, env_right, mixers, right_mas...]
    all_to_all x12 -> x0, local copies, waits for them, and re-layouts: 25.6 us -> none  [hamiltonian(): lax.all_to_all(half.reshape(1, rows, phys, width), 'tr', split_axis=3, co...]
    unnamed x36 -> x2, local copies, waits for them, and re-layouts: 22.6 us -> 3.34 us
    ppermute x4 -> x0, waiting for transfers between devices: 16.7 us -> none  [shifted(): return lax.ppermute(block, axis, route)]
    dot_general x12 -> x0, matrix products: 15.9 us -> none  [the longest x6 8.96 us: hamiltonian(): jnp.einsum('xc,ac->xa', mixed.reshape(rows * phys, width), env_left[chann...]
  transfers between devices with their start and end apart: 10 -> 0, of which waited for: 9 -> 0; matrix products, arithmetic and copies ran while one was open for 6% -> 0% of each run, Pallas kernels for 0% -> 0%
where the time goes in v1:
time: 137 us; the launch traced here: 135 us
  Pallas kernels  129 us (94%)
  local copies, waits for them, and re-layouts  3.34 us (2%)
  between operations  2.34 us (2%)
    pallas_call x1, Pallas kernels, body(): pl.pallas_call(kernel, out_shape=(jax.ShapeDtypeStruct(psi.shape, BF16),...  129 us
    unnamed x2, local copies, waits for them, and re-layouts  3.34 us

profile of v1, /device:TPU:1, one launch (start us, length us, event | category | flops | bytes accessed | tf_op | source)
XLA Modules:
  0.0 135.1 jit_solution(17701141283499157411)
XLA Ops:
  0.6 129.4 %shard_map.85 = (bf16[1,32,8,512]{3,2,1,0:T(8,128)(2,1)}, bf16[1,32,8,512]{3,2,1,0:T(8,128)(2,1)}, f32[1,1]{1,0:T(1,128)}) custom-call(bf16[1,32,8,512]{3,2,1,0:T(8,128)(2,1)} %psi_hbm.1, bf16[1,32,8,512]{3,2,1,0:T(8,128)(2,1)} %pc_hbm.1, bf16[3,1,512,512]{3,2,1,0:T(8,128)(2,1)} %left_hbm.1, bf16[3,1,512,512]{3,2,1,0:T(8,128)(2,1)} %right_hbm.1, ...), custom_call_target="tpu_custom_call" | custom-call | flops 2200000000 | bytes 2000000 | tf_op jit(solution)/shard_map/pallas_call | solution.py:688
  130.1 1.7 %copy.12 = bf16[1,32,8,512]{3,2,1,0:T(8,128)(2,1)} copy(bf16[1,32,8,512]{3,2,1,0:T(8,128)(2,1)} %get-tuple-element.12) | data formatting | bytes 524288
  131.7 1.7 %copy.13 = bf16[1,32,8,512]{3,2,1,0:T(8,128)(2,1)} copy(bf16[1,32,8,512]{3,2,1,0:T(8,128)(2,1)} %get-tuple-element.13) | data formatting | bytes 524288

commit v2 on v1

--- a/solution.py
+++ b/solution.py
@@ -17,7 +17,6 @@
 HALF = 256
 LINES = ROWS * PHYS
 COUNT = float(SEC * WIDTH * PHYS * WIDTH)
-STEPS = (1, 3, 2)
 
 
 def dot(a, b):
@@ -45,12 +44,10 @@
     return jnp.concatenate(pieces, axis=0)
 
 
-def columns_of(value):
-    blocks = []
+def store_columns(ref, value):
     for j in range(TR):
         p, side = divmod(j, 2)
-        blocks.append(value[p * ROWS : (p + 1) * ROWS, side * HALF : (side + 1) * HALF])
-    return jnp.stack(blocks, axis=0)
+        ref[j] = value[p * ROWS : (p + 1) * ROWS, side * HALF : (side + 1) * HALF]
 
 
 def kernel(
@@ -172,7 +169,7 @@
         load.start()
     gap = lax.rem(z - k + TR + 1, TR)
 
-    @pl.when(gap < 3)
+    @pl.when(gap < 4)
     def _():
         for load in env_loads:
             load.start()
@@ -223,7 +220,7 @@
     loads[0].wait()
     start = jnp.where(keep, psi_in[...].astype(F32).reshape(LINES, WIDTH), 0.0).astype(BF16)
     start_rows[...] = start
-    cols_send[...] = columns_of(to_phys_major(start).astype(BF16))
+    store_columns(cols_send, to_phys_major(start).astype(BF16))
     loads[1].wait()
     pc_send[...] = pc_in[...].astype(F32).reshape(TR, 2 * PHYS, WIDTH).astype(BF16)
 
@@ -254,7 +251,7 @@
             ring(lax.rem(z + 1, TR)),
         )
 
-    def move_in_ring(n, middle, target):
+    def ring_sends(n, middle, target, begin, end):
         def send(i, carry):
             peer = ring_peer(i)
 
@@ -267,8 +264,9 @@
             ).start()
             return carry
 
-        lax.fori_loop(0, TR - 1, send, 0)
-
+        lax.fori_loop(begin, end, send, 0)
+
+    def ring_rest(n, middle, target):
         @pl.when(z != k)
         def _():
             arrived(n, middle, z).wait_recv()
@@ -319,62 +317,68 @@
         ends.append(done)
         return done
 
-    def piece(m, i, rows=ROWS, first=0):
-        return env.at[m, :, pl.ds(pl.multiple_of(i * ROWS + first, 16), rows), :]
+    def env_matrix(m, c):
+        return env[m, c].reshape(WIDTH, WIDTH)
+
+    def piece(m, dy, dx, lanes=pl.ds(0, WIDTH)):
+        return env.at[m, :, lax.rem(y + dy + 4, 4), lax.rem(x + dx + 4, 4), :, lanes]
+
+    def row_set(m, dy, lanes):
+        return env.at[m, :, lax.rem(y + dy + 4, 4), :, :, lanes]
+
+    def column_set(m, dx, lanes):
+        return env.at[m, :, :, lax.rem(x + dx + 4, 4), :, lanes]
+
+    def scatter_copy(m, d, n):
+        return remote(
+            own_env.at[m, :, pl.ds((4 * d + n) * ROWS, ROWS), :],
+            land_env.at[m],
+            scatter_send_sem.at[m, n],
+            scatter_recv_sem.at[m],
+            plane(4 * d + n),
+        )
 
     def scatter(m):
         used = used_right if m == 0 else used_left
-        for d in range(3):
+        for d in range(4):
 
             @pl.when(gap == d)
             def _():
                 env_loads[m].wait()
-                for i in range(d, TR, 3):
-                    span = pl.ds(i * ROWS, ROWS)
-                    rows = own_env[m, :, span, :]
-                    own_env[m, :, span, :] = jnp.where(i * ROWS < used, rows, jnp.zeros_like(rows))
-
-                    @pl.when(k != i)
+                span = pl.ds(4 * d * ROWS, 4 * ROWS)
+                rows = own_env[m, :, span, :]
+                own_env[m, :, span, :] = jnp.where(4 * d * ROWS < used, rows, jnp.zeros_like(rows))
+                for n in range(4):
+
+                    @pl.when(k != 4 * d + n)
                     def _():
-                        remote(
-                            own_env.at[m, :, span, :],
-                            land_env.at[m],
-                            scatter_send_sem.at[m, i],
-                            scatter_recv_sem.at[m],
-                            plane(i),
-                        ).start()
-
-                    @pl.when(k == i)
+                        scatter_copy(m, d, n).start()
+
+                    @pl.when(k == 4 * d + n)
                     def _():
-                        land_env[m] = own_env[m, :, span, :]
+                        land_env[m] = own_env[m, :, pl.ds((4 * d + n) * ROWS, ROWS), :]
 
     def scatter_end(m):
-        for d in range(3):
+        for d in range(4):
 
             @pl.when(gap == d)
             def _():
-                for i in range(d, TR, 3):
-
-                    @pl.when(k != i)
+                for n in range(4):
+
+                    @pl.when(k != 4 * d + n)
                     def _():
-                        remote(
-                            own_env.at[m, :, pl.ds(i * ROWS, ROWS), :],
-                            land_env.at[m],
-                            scatter_send_sem.at[m, i],
-                            scatter_recv_sem.at[m],
-                            plane(i),
-                        ).wait_send()
-
-    shift = lax.rem(k, 3) - 1
+                        scatter_copy(m, d, n).wait_send()
+
+    shift = y - 1
     home = lax.rem(z - shift + TR, TR)
 
     def hand_over(m):
         return remote(
-            land_env.at[m], piece(m, k), own_send_sem.at[m], own_recv_sem.at[m], ring(home)
+            land_env.at[m], piece(m, 0, 0), own_send_sem.at[m], own_recv_sem.at[m], ring(home)
         )
 
     def keep_here(m):
-        return pltpu.make_async_copy(land_env.at[m], piece(m, k), own_recv_sem.at[m])
+        return pltpu.make_async_copy(land_env.at[m], piece(m, 0, 0), own_recv_sem.at[m])
 
     def own_start(m):
         @pl.when(home != k)
@@ -404,40 +408,59 @@
         def _():
             keep_here(m).wait()
 
-    def row_peer(step):
-        return 4 * y + lax.rem(x + step, 4)
-
-    def column_peer(step):
-        return 4 * lax.rem(y + step, 4) + x
-
-    def gather_copy(m, ref, i, side, target):
-        return remote(ref, ref, gather_send_sem.at[m], gather_recv_sem.at[m, i, side], plane(target))
-
-    def gather_direct(m):
-        for step in STEPS:
-            gather_copy(m, piece(m, k), k, 0, row_peer(step)).start()
-            gather_copy(m, piece(m, k), k, 0, column_peer(step)).start()
-
-    def gather_forward(m):
-        for step in STEPS:
-            source = row_peer(4 - step)
-            gather_copy(m, piece(m, source), source, 0, source).wait_recv()
-            for turn in STEPS:
-                gather_copy(m, piece(m, source, 16, 0), source, 0, column_peer(turn)).start()
-            source = column_peer(4 - step)
-            gather_copy(m, piece(m, source), source, 0, source).wait_recv()
-            for turn in STEPS:
-                gather_copy(m, piece(m, source, 16, 16), source, 1, row_peer(turn)).start()
+    first = pl.ds(0, HALF)
+    last = pl.ds(HALF, HALF)
+    quarters = [pl.ds(128 * n, 128) for n in range(4)]
+
+    def hop(m, n, ref, dy, dx):
+        target = 4 * lax.rem(y + dy + 4, 4) + lax.rem(x + dx + 4, 4)
+        return remote(ref, ref, gather_send_sem.at[m], gather_recv_sem.at[m, n], plane(target))
+
+    def gather_one(m):
+        own_wait(m)
+        hop(m, 0, piece(m, 0, 0, first), 0, 1).start()
+        hop(m, 1, piece(m, 0, 0, first), 0, -1).start()
+        hop(m, 2, piece(m, 0, 0, last), 1, 0).start()
+        hop(m, 3, piece(m, 0, 0, last), -1, 0).start()
+
+    def gather_two(m):
+        hop(m, 0, piece(m, 0, -1, first), 0, -1).wait_recv()
+        hop(m, 4, piece(m, 0, -1, quarters[0]), 0, 1).start()
+        hop(m, 1, piece(m, 0, 1, first), 0, 1).wait_recv()
+        hop(m, 5, piece(m, 0, 1, quarters[1]), 0, -1).start()
+        hop(m, 2, piece(m, -1, 0, last), -1, 0).wait_recv()
+        hop(m, 6, piece(m, -1, 0, quarters[2]), 1, 0).start()
+        hop(m, 3, piece(m, 1, 0, last), 1, 0).wait_recv()
+        hop(m, 7, piece(m, 1, 0, quarters[3]), -1, 0).start()
+
+    def gather_three(m):
+        hop(m, 4, piece(m, 0, 2, quarters[0]), 0, -1).wait_recv()
+        hop(m, 5, piece(m, 0, 2, quarters[1]), 0, 1).wait_recv()
+        hop(m, 8, row_set(m, 0, first), 1, 0).start()
+        hop(m, 9, row_set(m, 0, first), -1, 0).start()
+        hop(m, 6, piece(m, 2, 0, quarters[2]), -1, 0).wait_recv()
+        hop(m, 7, piece(m, 2, 0, quarters[3]), 1, 0).wait_recv()
+        hop(m, 10, column_set(m, 0, last), 0, 1).start()
+        hop(m, 11, column_set(m, 0, last), 0, -1).start()
+
+    def gather_four(m):
+        hop(m, 8, row_set(m, -1, first), -1, 0).wait_recv()
+        hop(m, 12, row_set(m, -1, quarters[0]), 1, 0).start()
+        hop(m, 9, row_set(m, 1, first), 1, 0).wait_recv()
+        hop(m, 13, row_set(m, 1, quarters[1]), -1, 0).start()
+        hop(m, 10, column_set(m, -1, last), 0, -1).wait_recv()
+        hop(m, 14, column_set(m, -1, quarters[2]), 0, 1).start()
+        hop(m, 11, column_set(m, 1, last), 0, 1).wait_recv()
+        hop(m, 15, column_set(m, 1, quarters[3]), 0, -1).start()
 
     def gather_wait(m):
-        for dy in STEPS:
-            for dx in STEPS:
-                source = 4 * lax.rem(y + dy, 4) + lax.rem(x + dx, 4)
-                gather_copy(m, piece(m, source, 16, 0), source, 0, source).wait_recv()
-                gather_copy(m, piece(m, source, 16, 16), source, 1, source).wait_recv()
+        hop(m, 12, row_set(m, 2, quarters[0]), -1, 0).wait_recv()
+        hop(m, 13, row_set(m, 2, quarters[1]), 1, 0).wait_recv()
+        hop(m, 14, column_set(m, 2, quarters[2]), 0, -1).wait_recv()
+        hop(m, 15, column_set(m, 2, quarters[3]), 0, 1).wait_recv()
 
     def gather_end(m):
-        sent = env.at[m, :, pl.ds(0, WIDTH - ROWS), :]
+        sent = own_env.at[m, :, pl.ds(0, WIDTH - ROWS), :]
         remote(
             sent, sent, gather_send_sem.at[m], own_recv_sem.at[m], ring(lax.rem(z + 1, TR))
         ).wait_send()
@@ -446,13 +469,21 @@
         def send(i, carry):
             peer = plane_peer(i)
             remote(
-                source.at[peer], target.at[k], turn_send_sem.at[n], turn_recv_sem.at[n], plane(peer)
+                source.at[:, peer],
+                target.at[:, k],
+                turn_send_sem.at[n],
+                turn_recv_sem.at[n],
+                plane(peer),
             ).start()
             return carry
 
         lax.fori_loop(1, TR, send, 0)
-        target[k] = source[k]
-        done = several(target, TR - 1, turn_send_sem.at[n], turn_recv_sem.at[n])
+        for place in range(2):
+            target[place, k] = source[place, k]
+        part = target.at[:, pl.ds(0, TR - 1)]
+        done = remote(
+            part, part, turn_send_sem.at[n], turn_recv_sem.at[n], ring(lax.rem(z + 1, TR))
+        )
         ends.append(done)
         return done
 
@@ -481,11 +512,11 @@
     scatter(0)
     scatter(1)
     own_start(0)
-    cols_done = move_in_ring(0, cols_mid, cols)
+    ring_sends(0, cols_mid, cols, 0, 7)
     own_start(1)
-    own_wait(0)
-    gather_direct(0)
-    move_in_plane(1, pc_send, pc_mid)
+    ring_sends(0, cols_mid, cols, 7, TR - 1)
+    cols_done = ring_rest(0, cols_mid, cols)
+    gather_one(0)
 
     wide_line = iota((WIDTH, WIDTH), 0)
     wide_other = iota((WIDTH, WIDTH), 1)
@@ -494,9 +525,11 @@
         return lax.rem(r, 32) // 2 * 32 + r // 32 * 2 + lax.rem(r, 2)
 
     to_new[...] = (old_row(wide_line) == wide_other).astype(BF16)
-    gather_forward(0)
-    own_wait(1)
-    gather_direct(1)
+    gather_two(0)
+    gather_one(1)
+    move_in_plane(1, pc_send, pc_mid)
+    gather_three(0)
+    gather_two(1)
     to_old[...] = (old_row(wide_other) == wide_line).astype(BF16)
     loads[2].wait()
     spread = ((iota((LINES, PHYS), 0) // ROWS) == iota((LINES, PHYS), 1)).astype(BF16)
@@ -504,6 +537,8 @@
     for c in range(3):
         mixed = dot_nt(dot(spread, mix[c]).astype(BF16), spread)
         kron[c] = jnp.where(same_row, mixed, 0.0).astype(BF16)
+    gather_three(1)
+    gather_four(0)
 
     cols_done.wait_recv()
     copies = shifts(0, cols, near_cols)
@@ -515,31 +550,32 @@
         return dot(to_new[...], value).astype(BF16).reshape(TR, ROWS, HALF)
 
     def right_part(c, value):
-        return reordered(dot(env[0, c], value).astype(BF16))
-
-    turn_send[0, :, 0] = right_part(0, own_cols)
-    turn_send[0, :, 1] = reordered(own_cols)
+        return reordered(dot(env_matrix(0, c), value).astype(BF16))
+
+    turn_send[0, 0] = right_part(0, own_cols)
+    turn_send[0, 1] = reordered(own_cols)
     turns.append(turn(0, turn_send.at[0], turn_recv.at[0]))
-    gather_forward(1)
+    gather_four(1)
     for way in range(2):
         copies[way].wait_recv()
-        turn_send[1, :, way] = right_part(
+        turn_send[1, way] = right_part(
             way + 1, inside(way, near_cols[way].reshape(WIDTH, HALF))
         )
     turns.append(turn(1, turn_send.at[1], turn_recv.at[1]))
-    pc_done = move_in_ring(1, pc_mid, pc_new)
+    ring_sends(1, pc_mid, pc_new, 0, TR - 1)
+    pc_done = ring_rest(1, pc_mid, pc_new)
     gather_wait(1)
     total = None
     for c, (group, place) in enumerate(((0, 0), (1, 0), (1, 1))):
         if place == 0:
             turns[group].wait_recv()
-        mixed = dot(kron[c], phys_major(turn_recv[group, :, place])).astype(BF16)
-        term = dot_nt(mixed, env[1, c])
+        mixed = dot(kron[c], phys_major(turn_recv[group, place])).astype(BF16)
+        term = dot_nt(mixed, env_matrix(1, c))
         total = term if total is None else total + term
     rounded = total.astype(BF16)
     first_send[...] = to_row_major(rounded).astype(BF16).reshape(TR, 2 * PHYS, WIDTH)
     image0 = rounded.astype(F32)
-    s = phys_major(turn_recv[0, :, 1]).astype(F32)
+    s = phys_major(turn_recv[0, 1]).astype(F32)
     pc_done.wait_recv()
     factors = to_phys_major(pc_new[...].reshape(LINES, WIDTH))
 
@@ -608,14 +644,14 @@
 
     def left_part(c, value):
         mixed = dot(kron[c], value).astype(BF16)
-        return columns_of(dot_nt(mixed, env[1, c]).astype(BF16))
-
-    half_send[0, :, 0] = left_part(0, trial_bf)
-    half_send[0, :, 1] = columns_of(trial_bf)
+        return dot_nt(mixed, env_matrix(1, c)).astype(BF16)
+
+    store_columns(half_send.at[0, 0], left_part(0, trial_bf))
+    store_columns(half_send.at[0, 1], trial_bf)
     turns.append(turn(2, half_send.at[0], half_recv.at[0]))
     for way in range(2):
         copies[way].wait_recv()
-        half_send[1, :, way] = left_part(way + 1, inside(way, near_vec[way]))
+        store_columns(half_send.at[1, way], left_part(way + 1, inside(way, near_vec[way])))
     turns.append(turn(3, half_send.at[1], half_recv.at[1]))
     second = trial_bf.astype(F32)
     tt = partial_sum(trial * trial)
@@ -624,13 +660,13 @@
     for c, (group, place) in enumerate(((0, 0), (1, 0), (1, 1))):
         if place == 0:
             turns[group].wait_recv()
-        half = dot(to_old[...], half_recv[group, :, place].reshape(WIDTH, HALF)).astype(BF16)
-        term = dot(env[0, c], half)
+        half = dot(to_old[...], half_recv[group, place].reshape(WIDTH, HALF)).astype(BF16)
+        term = dot(env_matrix(0, c), half)
         total = term if total is None else total + term
     second_send[...] = total.astype(BF16).reshape(TR, ROWS, HALF)
     back_in_ring(3, second_send, second_mid)
     image1_cols = total.astype(BF16).astype(F32)
-    trial_cols = dot(to_old[...], half_recv[0, :, 1].reshape(WIDTH, HALF))
+    trial_cols = dot(to_old[...], half_recv[0, 1].reshape(WIDTH, HALF))
     s1 = partial_sum(cols[...].reshape(WIDTH, HALF).astype(F32) * image1_cols)
     t1 = partial_sum(trial_cols * image1_cols)
     block = jnp.concatenate([tt, s1, t0, t1] * 2, axis=0)
@@ -683,7 +719,7 @@
     vmem = pl.BlockSpec(memory_space=pltpu.VMEM)
     dma = pltpu.SemaphoreType.DMA
     columns = (TR, ROWS, HALF)
-    pairs = (2, TR, 2, ROWS, HALF)
+    pairs = (2, 2, TR, ROWS, HALF)
     rows = (TR, 2 * PHYS, WIDTH)
     psi_new, residual_new, energy = pl.pallas_call(
         kernel,
@@ -701,7 +737,7 @@
             pltpu.SMEM((1, 2), jnp.int32),
             pltpu.VMEM((2, 3, WIDTH, WIDTH), BF16),
             pltpu.VMEM((2, 3, ROWS, WIDTH), BF16),
-            pltpu.VMEM((2, 3, WIDTH, WIDTH), BF16),
+            pltpu.VMEM((2, 3, 4, 4, ROWS, WIDTH), BF16),
             pltpu.VMEM((3, LINES, LINES), BF16),
             pltpu.VMEM((WIDTH, WIDTH), BF16),
             pltpu.VMEM((WIDTH, WIDTH), BF16),
@@ -729,12 +765,12 @@
             pltpu.VMEM((2, TR, 8, 128), F32),
             pltpu.VMEM((2, SEC, 8, 128), F32),
             dma((6,)),
-            dma((2, TR)),
+            dma((2, 4)),
             dma((2,)),
             dma((2,)),
             dma((2,)),
             dma((2,)),
-            dma((2, TR, 2)),
+            dma((2, 16)),
             dma((2, 2)),
             dma((2, 2)),
             dma((4,)),

time: 137 us -> 143 us (1.044)
  Pallas kernels: 129 us -> 135 us
    pallas_call x1, Pallas kernels: 129 us -> 135 us  [body(): pl.pallas_call(kernel, out_shape=(jax.ShapeDtypeStruct(psi.shape, BF16),...]
where the time goes in v2:
time: 143 us; the launch traced here: 141 us
  Pallas kernels  135 us (94%)
  local copies, waits for them, and re-layouts  3.34 us (2%)
  between operations  2.34 us (2%)
    pallas_call x1, Pallas kernels, body(): pl.pallas_call(kernel, out_shape=(jax.ShapeDtypeStruct(psi.shape, BF16),...  135 us
    unnamed x2, local copies, waits for them, and re-layouts  3.34 us

profile of v2, /device:TPU:1, one launch (start us, length us, event | category | flops | bytes accessed | tf_op | source)
XLA Modules:
  0.0 141.0 jit_solution(4496792467425183086)
XLA Ops:
  0.6 135.3 %shard_map.85 = (bf16[1,32,8,512]{3,2,1,0:T(8,128)(2,1)}, bf16[1,32,8,512]{3,2,1,0:T(8,128)(2,1)}, f32[1,1]{1,0:T(1,128)}) custom-call(bf16[1,32,8,512]{3,2,1,0:T(8,128)(2,1)} %psi_hbm.1, bf16[1,32,8,512]{3,2,1,0:T(8,128)(2,1)} %pc_hbm.1, bf16[3,1,512,512]{3,2,1,0:T(8,128)(2,1)} %left_hbm.1, bf16[3,1,512,512]{3,2,1,0:T(8,128)(2,1)} %right_hbm.1, ...), custom_call_target="tpu_custom_call" | custom-call | flops 2200000000 | bytes 2000000 | tf_op jit(solution)/shard_map/pallas_call | solution.py:724
  135.9 1.7 %copy.12 = bf16[1,32,8,512]{3,2,1,0:T(8,128)(2,1)} copy(bf16[1,32,8,512]{3,2,1,0:T(8,128)(2,1)} %get-tuple-element.12) | data formatting | bytes 524288
  137.6 1.7 %copy.13 = bf16[1,32,8,512]{3,2,1,0:T(8,128)(2,1)} copy(bf16[1,32,8,512]{3,2,1,0:T(8,128)(2,1)} %get-tuple-element.13) | data formatting | bytes 524288

commit v3 on v1

--- a/solution.py
+++ b/solution.py
@@ -45,12 +45,10 @@
     return jnp.concatenate(pieces, axis=0)
 
 
-def columns_of(value):
-    blocks = []
+def store_columns(ref, value):
     for j in range(TR):
         p, side = divmod(j, 2)
-        blocks.append(value[p * ROWS : (p + 1) * ROWS, side * HALF : (side + 1) * HALF])
-    return jnp.stack(blocks, axis=0)
+        ref[j] = value[p * ROWS : (p + 1) * ROWS, side * HALF : (side + 1) * HALF]
 
 
 def kernel(
@@ -88,10 +86,8 @@
     half_send,
     half_recv,
     first_send,
-    first_mid,
     first_old,
     second_send,
-    second_mid,
     second_old,
     red_send,
     red_tr,
@@ -196,8 +192,21 @@
         device_id={"tr": lax.rem(z + 2 * core - 1 + TR, TR), "sec": partner},
         device_id_type=MESH,
     )
+    def greet_far(j, carry):
+        @pl.when((k != z) | (j != k))
+        def _():
+            pl.semaphore_signal(
+                barrier,
+                inc=1,
+                device_id={"tr": k, "sec": 2 * j + core},
+                device_id_type=MESH,
+            )
+
+        return carry
+
     lax.fori_loop(1, SEC, greet_sec, 0)
     lax.fori_loop(1, TR, greet_tr, 0)
+    lax.fori_loop(0, TR, greet_far, 0)
 
     line = iota((LINES, LINES), 0)
     other = iota((LINES, LINES), 1)
@@ -223,11 +232,11 @@
     loads[0].wait()
     start = jnp.where(keep, psi_in[...].astype(F32).reshape(LINES, WIDTH), 0.0).astype(BF16)
     start_rows[...] = start
-    cols_send[...] = columns_of(to_phys_major(start).astype(BF16))
+    store_columns(cols_send, to_phys_major(start).astype(BF16))
     loads[1].wait()
     pc_send[...] = pc_in[...].astype(F32).reshape(TR, 2 * PHYS, WIDTH).astype(BF16)
 
-    pl.semaphore_wait(barrier, TR + SEC - 1)
+    pl.semaphore_wait(barrier, TR + SEC - 1 + TR - jnp.where(k == z, 1, 0))
 
     def move_in_plane(n, source, middle):
         def send(i, carry):
@@ -278,46 +287,45 @@
         ends.append(done)
         return done
 
-    def back_in_ring(n, source, middle):
+    def back(n, source, target, begin, end):
         def send(i, carry):
             peer = ring_peer(i)
             remote(
                 source.at[peer],
-                middle.at[z],
+                target.at[k],
                 move_send_sem.at[n, 0],
-                move_one_sem.at[n, z],
-                ring(peer),
+                move_two_sem.at[n],
+                {"tr": peer, "sec": 2 * z + core},
             ).start()
             return carry
 
-        lax.fori_loop(0, TR - 1, send, 0)
-        middle[z] = source[z]
-        ends.append(several(middle, TR - 1, move_send_sem.at[n, 0], move_two_sem.at[n]))
-
-    def back_in_plane(n, middle, target):
-        def forward(index):
-            @pl.when(index != k)
+        lax.fori_loop(begin, end, send, 0)
+
+    def back_home(n, source, target):
+        @pl.when(z != k)
+        def _():
+            remote(
+                source.at[z],
+                target.at[k],
+                move_send_sem.at[n, 0],
+                move_two_sem.at[n],
+                {"tr": z, "sec": 2 * z + core},
+            ).start()
+
+        @pl.when(z == k)
+        def _():
+            target[k] = source[k]
+
+    def back_wait(n, target, sent):
+        for same in range(2):
+
+            @pl.when((z == k) if same else (z != k))
             def _():
-                remote(
-                    middle.at[index],
-                    target.at[k],
-                    move_send_sem.at[n, 1],
-                    move_two_sem.at[n],
-                    plane(index),
-                ).start()
-
-        def send(i, carry):
-            index = ring_source(i)
-            arrived(n, middle, index).wait_recv()
-            forward(index)
-            return carry
-
-        forward(z)
-        lax.fori_loop(0, TR - 1, send, 0)
-        target[k] = middle[k]
-        done = several(target, TR - 1, move_send_sem.at[n, 1], move_two_sem.at[n])
-        ends.append(done)
-        return done
+                done = several(target, TR - same, move_send_sem.at[n, 0], move_two_sem.at[n])
+                if sent:
+                    done.wait_send()
+                else:
+                    done.wait_recv()
 
     def piece(m, i, rows=ROWS, first=0):
         return env.at[m, :, pl.ds(pl.multiple_of(i * ROWS + first, 16), rows), :]
@@ -446,13 +454,21 @@
         def send(i, carry):
             peer = plane_peer(i)
             remote(
-                source.at[peer], target.at[k], turn_send_sem.at[n], turn_recv_sem.at[n], plane(peer)
+                source.at[:, peer],
+                target.at[:, k],
+                turn_send_sem.at[n],
+                turn_recv_sem.at[n],
+                plane(peer),
             ).start()
             return carry
 
         lax.fori_loop(1, TR, send, 0)
-        target[k] = source[k]
-        done = several(target, TR - 1, turn_send_sem.at[n], turn_recv_sem.at[n])
+        for place in range(2):
+            target[place, k] = source[place, k]
+        part = target.at[:, pl.ds(0, TR - 1)]
+        done = remote(
+            part, part, turn_send_sem.at[n], turn_recv_sem.at[n], ring(lax.rem(z + 1, TR))
+        )
         ends.append(done)
         return done
 
@@ -517,13 +533,13 @@
     def right_part(c, value):
         return reordered(dot(env[0, c], value).astype(BF16))
 
-    turn_send[0, :, 0] = right_part(0, own_cols)
-    turn_send[0, :, 1] = reordered(own_cols)
+    turn_send[0, 0] = right_part(0, own_cols)
+    turn_send[0, 1] = reordered(own_cols)
     turns.append(turn(0, turn_send.at[0], turn_recv.at[0]))
     gather_forward(1)
     for way in range(2):
         copies[way].wait_recv()
-        turn_send[1, :, way] = right_part(
+        turn_send[1, way] = right_part(
             way + 1, inside(way, near_cols[way].reshape(WIDTH, HALF))
         )
     turns.append(turn(1, turn_send.at[1], turn_recv.at[1]))
@@ -533,13 +549,13 @@
     for c, (group, place) in enumerate(((0, 0), (1, 0), (1, 1))):
         if place == 0:
             turns[group].wait_recv()
-        mixed = dot(kron[c], phys_major(turn_recv[group, :, place])).astype(BF16)
+        mixed = dot(kron[c], phys_major(turn_recv[group, place])).astype(BF16)
         term = dot_nt(mixed, env[1, c])
         total = term if total is None else total + term
     rounded = total.astype(BF16)
     first_send[...] = to_row_major(rounded).astype(BF16).reshape(TR, 2 * PHYS, WIDTH)
     image0 = rounded.astype(F32)
-    s = phys_major(turn_recv[0, :, 1]).astype(F32)
+    s = phys_major(turn_recv[0, 1]).astype(F32)
     pc_done.wait_recv()
     factors = to_phys_major(pc_new[...].reshape(LINES, WIDTH))
 
@@ -589,8 +605,9 @@
     parts = (s * s, s * image0, weighted * image0, weighted * s)
     block = jnp.concatenate([partial_sum(part) for part in parts] * 2, axis=0)
     tr_start(0, block).wait_recv()
-    back_in_ring(2, first_send, first_mid)
-    sec_start(0, jnp.sum(red_tr[0], axis=0)).wait_recv()
+    sums_done = sec_start(0, jnp.sum(red_tr[0], axis=0))
+    back(2, first_send, first_old, 0, 5)
+    sums_done.wait_recv()
     ss, sw, spw, sps = means(jnp.sum(red_sec[0], axis=0))
     norm = lax.rsqrt(ss + EPSILON)
     theta = norm * norm * sw
@@ -608,15 +625,17 @@
 
     def left_part(c, value):
         mixed = dot(kron[c], value).astype(BF16)
-        return columns_of(dot_nt(mixed, env[1, c]).astype(BF16))
-
-    half_send[0, :, 0] = left_part(0, trial_bf)
-    half_send[0, :, 1] = columns_of(trial_bf)
+        return dot_nt(mixed, env[1, c]).astype(BF16)
+
+    store_columns(half_send.at[0, 0], left_part(0, trial_bf))
+    store_columns(half_send.at[0, 1], trial_bf)
     turns.append(turn(2, half_send.at[0], half_recv.at[0]))
     for way in range(2):
         copies[way].wait_recv()
-        half_send[1, :, way] = left_part(way + 1, inside(way, near_vec[way]))
+        store_columns(half_send.at[1, way], left_part(way + 1, inside(way, near_vec[way])))
     turns.append(turn(3, half_send.at[1], half_recv.at[1]))
+    back(2, first_send, first_old, 5, TR - 1)
+    back_home(2, first_send, first_old)
     second = trial_bf.astype(F32)
     tt = partial_sum(trial * trial)
     t0 = partial_sum(second * image0)
@@ -624,20 +643,19 @@
     for c, (group, place) in enumerate(((0, 0), (1, 0), (1, 1))):
         if place == 0:
             turns[group].wait_recv()
-        half = dot(to_old[...], half_recv[group, :, place].reshape(WIDTH, HALF)).astype(BF16)
+        half = dot(to_old[...], half_recv[group, place].reshape(WIDTH, HALF)).astype(BF16)
         term = dot(env[0, c], half)
         total = term if total is None else total + term
     second_send[...] = total.astype(BF16).reshape(TR, ROWS, HALF)
-    back_in_ring(3, second_send, second_mid)
+    back(3, second_send, second_old, 0, TR - 1)
+    back_home(3, second_send, second_old)
     image1_cols = total.astype(BF16).astype(F32)
-    trial_cols = dot(to_old[...], half_recv[0, :, 1].reshape(WIDTH, HALF))
+    trial_cols = dot(to_old[...], half_recv[0, 1].reshape(WIDTH, HALF))
     s1 = partial_sum(cols[...].reshape(WIDTH, HALF).astype(F32) * image1_cols)
     t1 = partial_sum(trial_cols * image1_cols)
     block = jnp.concatenate([tt, s1, t0, t1] * 2, axis=0)
     sec_start(1, block).wait_recv()
     sums_done = tr_start(1, jnp.sum(red_sec[1], axis=0))
-    first_done = back_in_plane(2, first_mid, first_old)
-    second_done = back_in_plane(3, second_mid, second_old)
     sums_done.wait_recv()
     tt, s1, t0, t1 = means(jnp.sum(red_tr[1], axis=0))
 
@@ -654,7 +672,7 @@
     two = weight_two * scale * grow
     energy_out[...] = energy
 
-    first_done.wait_recv()
+    back_wait(2, first_old, False)
     old_image = first_old[...].reshape(LINES, WIDTH).astype(F32)
     old_start = start_rows[...].astype(F32)
     old_factors = pc_send[...].reshape(LINES, WIDTH).astype(F32)
@@ -662,7 +680,7 @@
     ritz = one * old_start + two * old_trial
     psi_out[...] = ritz.reshape(ROWS, PHYS, WIDTH).astype(BF16)[None]
     partial = one * old_image - energy * ritz
-    second_done.wait_recv()
+    back_wait(3, second_old, False)
     residual = partial + two * to_row_major(phys_major(second_old[...]))
     res_out[...] = residual.reshape(ROWS, PHYS, WIDTH).astype(BF16)[None]
 
@@ -674,6 +692,8 @@
         def _():
             hand_over(m).wait_send()
 
+    back_wait(2, first_old, True)
+    back_wait(3, second_old, True)
     for end in ends:
         end.wait_send()
 
@@ -683,7 +703,7 @@
     vmem = pl.BlockSpec(memory_space=pltpu.VMEM)
     dma = pltpu.SemaphoreType.DMA
     columns = (TR, ROWS, HALF)
-    pairs = (2, TR, 2, ROWS, HALF)
+    pairs = (2, 2, TR, ROWS, HALF)
     rows = (TR, 2 * PHYS, WIDTH)
     psi_new, residual_new, energy = pl.pallas_call(
         kernel,
@@ -721,8 +741,6 @@
             pltpu.VMEM(pairs, BF16),
             pltpu.VMEM(rows, BF16),
             pltpu.VMEM(rows, BF16),
-            pltpu.VMEM(rows, BF16),
-            pltpu.VMEM(columns, BF16),
             pltpu.VMEM(columns, BF16),
             pltpu.VMEM(columns, BF16),
             pltpu.VMEM((2, 2, 8, 128), F32),

time: 137 us -> 140 us (1.022)
  Pallas kernels: 129 us -> 132 us
    pallas_call x1, Pallas kernels: 129 us -> 132 us  [body(): pl.pallas_call(kernel, out_shape=(jax.ShapeDtypeStruct(psi.shape, BF16),...]
where the time goes in v3:
time: 140 us; the launch traced here: 138 us
  Pallas kernels  132 us (94%)
  local copies, waits for them, and re-layouts  3.34 us (2%)
  between operations  2.34 us (2%)
    pallas_call x1, Pallas kernels, body(): pl.pallas_call(kernel, out_shape=(jax.ShapeDtypeStruct(psi.shape, BF16),...  132 us
    unnamed x2, local copies, waits for them, and re-layouts  3.34 us

profile of v3, /device:TPU:1, one launch (start us, length us, event | category | flops | bytes accessed | tf_op | source)
XLA Modules:
  0.0 137.7 jit_solution(2837041202009182528)
XLA Ops:
  0.6 132.0 %shard_map.85 = (bf16[1,32,8,512]{3,2,1,0:T(8,128)(2,1)}, bf16[1,32,8,512]{3,2,1,0:T(8,128)(2,1)}, f32[1,1]{1,0:T(1,128)}) custom-call(bf16[1,32,8,512]{3,2,1,0:T(8,128)(2,1)} %psi_hbm.1, bf16[1,32,8,512]{3,2,1,0:T(8,128)(2,1)} %pc_hbm.1, bf16[3,1,512,512]{3,2,1,0:T(8,128)(2,1)} %left_hbm.1, bf16[3,1,512,512]{3,2,1,0:T(8,128)(2,1)} %right_hbm.1, ...), custom_call_target="tpu_custom_call" | custom-call | flops 2200000000 | bytes 2000000 | tf_op jit(solution)/shard_map/pallas_call | solution.py:708
  132.7 1.7 %copy.12 = bf16[1,32,8,512]{3,2,1,0:T(8,128)(2,1)} copy(bf16[1,32,8,512]{3,2,1,0:T(8,128)(2,1)} %get-tuple-element.12) | data formatting | bytes 524288
  134.3 1.7 %copy.13 = bf16[1,32,8,512]{3,2,1,0:T(8,128)(2,1)} copy(bf16[1,32,8,512]{3,2,1,0:T(8,128)(2,1)} %get-tuple-element.13) | data formatting | bytes 524288

commit v4 on v2

--- a/solution.py
+++ b/solution.py
@@ -17,6 +17,7 @@
 HALF = 256
 LINES = ROWS * PHYS
 COUNT = float(SEC * WIDTH * PHYS * WIDTH)
+STEPS = (1, 3, 2)
 
 
 def dot(a, b):
@@ -85,10 +86,8 @@
     half_send,
     half_recv,
     first_send,
-    first_mid,
     first_old,
     second_send,
-    second_mid,
     second_old,
     red_send,
     red_tr,
@@ -193,8 +192,21 @@
         device_id={"tr": lax.rem(z + 2 * core - 1 + TR, TR), "sec": partner},
         device_id_type=MESH,
     )
+    def greet_far(j, carry):
+        @pl.when((k != z) | (j != k))
+        def _():
+            pl.semaphore_signal(
+                barrier,
+                inc=1,
+                device_id={"tr": k, "sec": 2 * j + core},
+                device_id_type=MESH,
+            )
+
+        return carry
+
     lax.fori_loop(1, SEC, greet_sec, 0)
     lax.fori_loop(1, TR, greet_tr, 0)
+    lax.fori_loop(0, TR, greet_far, 0)
 
     line = iota((LINES, LINES), 0)
     other = iota((LINES, LINES), 1)
@@ -224,7 +236,7 @@
     loads[1].wait()
     pc_send[...] = pc_in[...].astype(F32).reshape(TR, 2 * PHYS, WIDTH).astype(BF16)
 
-    pl.semaphore_wait(barrier, TR + SEC - 1)
+    pl.semaphore_wait(barrier, TR + SEC - 1 + TR - jnp.where(k == z, 1, 0))
 
     def move_in_plane(n, source, middle):
         def send(i, carry):
@@ -251,7 +263,7 @@
             ring(lax.rem(z + 1, TR)),
         )
 
-    def ring_sends(n, middle, target, begin, end):
+    def move_in_ring(n, middle, target):
         def send(i, carry):
             peer = ring_peer(i)
 
@@ -264,9 +276,8 @@
             ).start()
             return carry
 
-        lax.fori_loop(begin, end, send, 0)
-
-    def ring_rest(n, middle, target):
+        lax.fori_loop(0, TR - 1, send, 0)
+
         @pl.when(z != k)
         def _():
             arrived(n, middle, z).wait_recv()
@@ -276,58 +287,57 @@
         ends.append(done)
         return done
 
-    def back_in_ring(n, source, middle):
+    def back(n, source, target, begin, end):
         def send(i, carry):
             peer = ring_peer(i)
             remote(
                 source.at[peer],
-                middle.at[z],
+                target.at[k],
                 move_send_sem.at[n, 0],
-                move_one_sem.at[n, z],
-                ring(peer),
+                move_two_sem.at[n],
+                {"tr": peer, "sec": 2 * z + core},
             ).start()
             return carry
 
-        lax.fori_loop(0, TR - 1, send, 0)
-        middle[z] = source[z]
-        ends.append(several(middle, TR - 1, move_send_sem.at[n, 0], move_two_sem.at[n]))
-
-    def back_in_plane(n, middle, target):
-        def forward(index):
-            @pl.when(index != k)
+        lax.fori_loop(begin, end, send, 0)
+
+    def back_home(n, source, target):
+        @pl.when(z != k)
+        def _():
+            remote(
+                source.at[z],
+                target.at[k],
+                move_send_sem.at[n, 0],
+                move_two_sem.at[n],
+                {"tr": z, "sec": 2 * z + core},
+            ).start()
+
+        @pl.when(z == k)
+        def _():
+            target[k] = source[k]
+
+    def back_wait(n, target, sent):
+        for same in range(2):
+
+            @pl.when((z == k) if same else (z != k))
             def _():
-                remote(
-                    middle.at[index],
-                    target.at[k],
-                    move_send_sem.at[n, 1],
-                    move_two_sem.at[n],
-                    plane(index),
-                ).start()
-
-        def send(i, carry):
-            index = ring_source(i)
-            arrived(n, middle, index).wait_recv()
-            forward(index)
-            return carry
-
-        forward(z)
-        lax.fori_loop(0, TR - 1, send, 0)
-        target[k] = middle[k]
-        done = several(target, TR - 1, move_send_sem.at[n, 1], move_two_sem.at[n])
-        ends.append(done)
-        return done
+                done = several(target, TR - same, move_send_sem.at[n, 0], move_two_sem.at[n])
+                if sent:
+                    done.wait_send()
+                else:
+                    done.wait_recv()
 
     def env_matrix(m, c):
         return env[m, c].reshape(WIDTH, WIDTH)
 
-    def piece(m, dy, dx, lanes=pl.ds(0, WIDTH)):
-        return env.at[m, :, lax.rem(y + dy + 4, 4), lax.rem(x + dx + 4, 4), :, lanes]
-
-    def row_set(m, dy, lanes):
-        return env.at[m, :, lax.rem(y + dy + 4, 4), :, :, lanes]
-
-    def column_set(m, dx, lanes):
-        return env.at[m, :, :, lax.rem(x + dx + 4, 4), :, lanes]
+    def piece(m, dy, dx, part=(pl.ds(0, ROWS), pl.ds(0, WIDTH))):
+        return env.at[m, :, lax.rem(y + dy + 4, 4), lax.rem(x + dx + 4, 4), part[0], part[1]]
+
+    def row_set(m, dy, part):
+        return env.at[m, :, lax.rem(y + dy + 4, 4), :, part[0], part[1]]
+
+    def column_set(m, dx, part):
+        return env.at[m, :, :, lax.rem(x + dx + 4, 4), part[0], part[1]]
 
     def scatter_copy(m, d, n):
         return remote(
@@ -408,9 +418,9 @@
         def _():
             keep_here(m).wait()
 
-    first = pl.ds(0, HALF)
-    last = pl.ds(HALF, HALF)
-    quarters = [pl.ds(128 * n, 128) for n in range(4)]
+    first = (pl.ds(0, 16), pl.ds(0, WIDTH))
+    last = (pl.ds(16, 16), pl.ds(0, WIDTH))
+    quarters = [(pl.ds(n // 2 * 16, 16), pl.ds(n % 2 * HALF, HALF)) for n in range(4)]
 
     def hop(m, n, ref, dy, dx):
         target = 4 * lax.rem(y + dy + 4, 4) + lax.rem(x + dx + 4, 4)
@@ -465,7 +475,10 @@
             sent, sent, gather_send_sem.at[m], own_recv_sem.at[m], ring(lax.rem(z + 1, TR))
         ).wait_send()
 
-    def turn(n, source, target):
+    def turn(n, sources, targets, begin, count):
+        source = sources.at[pl.ds(begin, count)]
+        target = targets.at[pl.ds(begin, count)]
+
         def send(i, carry):
             peer = plane_peer(i)
             remote(
@@ -478,8 +491,8 @@
             return carry
 
         lax.fori_loop(1, TR, send, 0)
-        for place in range(2):
-            target[place, k] = source[place, k]
+        for place in range(begin, begin + count):
+            targets[place, k] = sources[place, k]
         part = target.at[:, pl.ds(0, TR - 1)]
         done = remote(
             part, part, turn_send_sem.at[n], turn_recv_sem.at[n], ring(lax.rem(z + 1, TR))
@@ -510,13 +523,11 @@
 
     move_in_plane(0, cols_send, cols_mid)
     scatter(0)
+    own_start(0)
+    cols_done = move_in_ring(0, cols_mid, cols)
     scatter(1)
-    own_start(0)
-    ring_sends(0, cols_mid, cols, 0, 7)
-    own_start(1)
-    ring_sends(0, cols_mid, cols, 7, TR - 1)
-    cols_done = ring_rest(0, cols_mid, cols)
     gather_one(0)
+    move_in_plane(1, pc_send, pc_mid)
 
     wide_line = iota((WIDTH, WIDTH), 0)
     wide_other = iota((WIDTH, WIDTH), 1)
@@ -526,10 +537,6 @@
 
     to_new[...] = (old_row(wide_line) == wide_other).astype(BF16)
     gather_two(0)
-    gather_one(1)
-    move_in_plane(1, pc_send, pc_mid)
-    gather_three(0)
-    gather_two(1)
     to_old[...] = (old_row(wide_other) == wide_line).astype(BF16)
     loads[2].wait()
     spread = ((iota((LINES, PHYS), 0) // ROWS) == iota((LINES, PHYS), 1)).astype(BF16)
@@ -537,45 +544,48 @@
     for c in range(3):
         mixed = dot_nt(dot(spread, mix[c]).astype(BF16), spread)
         kron[c] = jnp.where(same_row, mixed, 0.0).astype(BF16)
-    gather_three(1)
-    gather_four(0)
+    own_start(1)
+    gather_three(0)
+
+    def reordered(value):
+        return dot(to_new[...], value).astype(BF16).reshape(TR, ROWS, HALF)
+
+    def right_part(c, value):
+        return reordered(dot(env_matrix(0, c), value).astype(BF16))
 
     cols_done.wait_recv()
     copies = shifts(0, cols, near_cols)
     own_cols = cols[...].reshape(WIDTH, HALF)
+    turn_send[3] = reordered(own_cols)
+    start_turn = turn(2, turn_send, turn_recv, 3, 1)
+    gather_four(0)
+    gather_one(1)
     gather_wait(0)
-    turns = []
-
-    def reordered(value):
-        return dot(to_new[...], value).astype(BF16).reshape(TR, ROWS, HALF)
-
-    def right_part(c, value):
-        return reordered(dot(env_matrix(0, c), value).astype(BF16))
-
-    turn_send[0, 0] = right_part(0, own_cols)
-    turn_send[0, 1] = reordered(own_cols)
-    turns.append(turn(0, turn_send.at[0], turn_recv.at[0]))
-    gather_four(1)
+    turn_send[0] = right_part(0, own_cols)
+    turns = [turn(0, turn_send, turn_recv, 0, 1)]
+    gather_two(1)
     for way in range(2):
         copies[way].wait_recv()
-        turn_send[1, way] = right_part(
+        turn_send[way + 1] = right_part(
             way + 1, inside(way, near_cols[way].reshape(WIDTH, HALF))
         )
-    turns.append(turn(1, turn_send.at[1], turn_recv.at[1]))
-    ring_sends(1, pc_mid, pc_new, 0, TR - 1)
-    pc_done = ring_rest(1, pc_mid, pc_new)
+    turns.append(turn(1, turn_send, turn_recv, 1, 2))
+    gather_three(1)
+    pc_done = move_in_ring(1, pc_mid, pc_new)
+    gather_four(1)
     gather_wait(1)
     total = None
-    for c, (group, place) in enumerate(((0, 0), (1, 0), (1, 1))):
-        if place == 0:
-            turns[group].wait_recv()
-        mixed = dot(kron[c], phys_major(turn_recv[group, place])).astype(BF16)
+    for c in range(3):
+        if c < 2:
+            turns[c].wait_recv()
+        mixed = dot(kron[c], phys_major(turn_recv[c])).astype(BF16)
         term = dot_nt(mixed, env_matrix(1, c))
         total = term if total is None else total + term
     rounded = total.astype(BF16)
     first_send[...] = to_row_major(rounded).astype(BF16).reshape(TR, 2 * PHYS, WIDTH)
     image0 = rounded.astype(F32)
-    s = phys_major(turn_recv[0, 1]).astype(F32)
+    start_turn.wait_recv()
+    s = phys_major(turn_recv[3]).astype(F32)
     pc_done.wait_recv()
     factors = to_phys_major(pc_new[...].reshape(LINES, WIDTH))
 
@@ -625,8 +635,9 @@
     parts = (s * s, s * image0, weighted * image0, weighted * s)
     block = jnp.concatenate([partial_sum(part) for part in parts] * 2, axis=0)
     tr_start(0, block).wait_recv()
-    back_in_ring(2, first_send, first_mid)
-    sec_start(0, jnp.sum(red_tr[0], axis=0)).wait_recv()
+    sums_done = sec_start(0, jnp.sum(red_tr[0], axis=0))
+    back(2, first_send, first_old, 0, 5)
+    sums_done.wait_recv()
     ss, sw, spw, sps = means(jnp.sum(red_sec[0], axis=0))
     norm = lax.rsqrt(ss + EPSILON)
     theta = norm * norm * sw
@@ -646,34 +657,37 @@
         mixed = dot(kron[c], value).astype(BF16)
         return dot_nt(mixed, env_matrix(1, c)).astype(BF16)
 
-    store_columns(half_send.at[0, 0], left_part(0, trial_bf))
-    store_columns(half_send.at[0, 1], trial_bf)
-    turns.append(turn(2, half_send.at[0], half_recv.at[0]))
+    store_columns(half_send.at[0], left_part(0, trial_bf))
+    turns = [turn(3, half_send, half_recv, 0, 1)]
+    store_columns(half_send.at[3], trial_bf)
     for way in range(2):
         copies[way].wait_recv()
-        store_columns(half_send.at[1, way], left_part(way + 1, inside(way, near_vec[way])))
-    turns.append(turn(3, half_send.at[1], half_recv.at[1]))
+        store_columns(half_send.at[way + 1], left_part(way + 1, inside(way, near_vec[way])))
+    turns.append(turn(4, half_send, half_recv, 1, 2))
+    trial_turn = turn(5, half_send, half_recv, 3, 1)
+    back(2, first_send, first_old, 5, TR - 1)
+    back_home(2, first_send, first_old)
     second = trial_bf.astype(F32)
     tt = partial_sum(trial * trial)
     t0 = partial_sum(second * image0)
     total = None
-    for c, (group, place) in enumerate(((0, 0), (1, 0), (1, 1))):
-        if place == 0:
-            turns[group].wait_recv()
-        half = dot(to_old[...], half_recv[group, place].reshape(WIDTH, HALF)).astype(BF16)
+    for c in range(3):
+        if c < 2:
+            turns[c].wait_recv()
+        half = dot(to_old[...], half_recv[c].reshape(WIDTH, HALF)).astype(BF16)
         term = dot(env_matrix(0, c), half)
         total = term if total is None else total + term
     second_send[...] = total.astype(BF16).reshape(TR, ROWS, HALF)
-    back_in_ring(3, second_send, second_mid)
+    back(3, second_send, second_old, 0, TR - 1)
+    back_home(3, second_send, second_old)
     image1_cols = total.astype(BF16).astype(F32)
-    trial_cols = dot(to_old[...], half_recv[0, 1].reshape(WIDTH, HALF))
+    trial_turn.wait_recv()
+    trial_cols = dot(to_old[...], half_recv[3].reshape(WIDTH, HALF))
     s1 = partial_sum(cols[...].reshape(WIDTH, HALF).astype(F32) * image1_cols)
     t1 = partial_sum(trial_cols * image1_cols)
     block = jnp.concatenate([tt, s1, t0, t1] * 2, axis=0)
     sec_start(1, block).wait_recv()
     sums_done = tr_start(1, jnp.sum(red_sec[1], axis=0))
-    first_done = back_in_plane(2, first_mid, first_old)
-    second_done = back_in_plane(3, second_mid, second_old)
     sums_done.wait_recv()
     tt, s1, t0, t1 = means(jnp.sum(red_tr[1], axis=0))
 
@@ -690,7 +704,7 @@
     two = weight_two * scale * grow
     energy_out[...] = energy
 
-    first_done.wait_recv()
+    back_wait(2, first_old, False)
     old_image = first_old[...].reshape(LINES, WIDTH).astype(F32)
     old_start = start_rows[...].astype(F32)
     old_factors = pc_send[...].reshape(LINES, WIDTH).astype(F32)
@@ -698,7 +712,7 @@
     ritz = one * old_start + two * old_trial
     psi_out[...] = ritz.reshape(ROWS, PHYS, WIDTH).astype(BF16)[None]
     partial = one * old_image - energy * ritz
-    second_done.wait_recv()
+    back_wait(3, second_old, False)
     residual = partial + two * to_row_major(phys_major(second_old[...]))
     res_out[...] = residual.reshape(ROWS, PHYS, WIDTH).astype(BF16)[None]
 
@@ -710,6 +724,8 @@
         def _():
             hand_over(m).wait_send()
 
+    back_wait(2, first_old, True)
+    back_wait(3, second_old, True)
     for end in ends:
         end.wait_send()
 
@@ -719,7 +735,7 @@
     vmem = pl.BlockSpec(memory_space=pltpu.VMEM)
     dma = pltpu.SemaphoreType.DMA
     columns = (TR, ROWS, HALF)
-    pairs = (2, 2, TR, ROWS, HALF)
+    fours = (4, TR, ROWS, HALF)
     rows = (TR, 2 * PHYS, WIDTH)
     psi_new, residual_new, energy = pl.pallas_call(
         kernel,
@@ -746,19 +762,17 @@
             pltpu.VMEM(columns, BF16),
             pltpu.VMEM(columns, BF16),
             pltpu.VMEM((2, *columns), BF16),
-            pltpu.VMEM(pairs, BF16),
-            pltpu.VMEM(pairs, BF16),
+            pltpu.VMEM(fours, BF16),
+            pltpu.VMEM(fours, BF16),
             pltpu.VMEM(rows, BF16),
             pltpu.VMEM(rows, BF16),
             pltpu.VMEM(rows, BF16),
             pltpu.VMEM((LINES, WIDTH), BF16),
             pltpu.VMEM((2, LINES, WIDTH), BF16),
-            pltpu.VMEM(pairs, BF16),
-            pltpu.VMEM(pairs, BF16),
+            pltpu.VMEM(fours, BF16),
+            pltpu.VMEM(fours, BF16),
             pltpu.VMEM(rows, BF16),
             pltpu.VMEM(rows, BF16),
-            pltpu.VMEM(rows, BF16),
-            pltpu.VMEM(columns, BF16),
             pltpu.VMEM(columns, BF16),
             pltpu.VMEM(columns, BF16),
             pltpu.VMEM((2, 2, 8, 128), F32),
@@ -773,8 +787,8 @@
             dma((2, 16)),
             dma((2, 2)),
             dma((2, 2)),
-            dma((4,)),
-            dma((4,)),
+            dma((6,)),
+            dma((6,)),
             dma((4, 2)),
             dma((4, TR)),
             dma((4,)),

time: 143 us -> 139 us (0.972); the launches traced: 141 us -> 139 us
  Pallas kernels: 135 us -> 133 us
    pallas_call x1, Pallas kernels: 135 us -> 133 us  [body(): pl.pallas_call(kernel, out_shape=(jax.ShapeDtypeStruct(psi.shape, BF16),...]
where the time goes in v4:
time: 139 us
  Pallas kernels  133 us (96%)
  local copies, waits for them, and re-layouts  3.34 us (2%)
  between operations  2.34 us (2%)
    pallas_call x1, Pallas kernels, body(): pl.pallas_call(kernel, out_shape=(jax.ShapeDtypeStruct(psi.shape, BF16),...  133 us
    unnamed x2, local copies, waits for them, and re-layouts  3.34 us

profile of v4, /device:TPU:1, one launch (start us, length us, event | category | flops | bytes accessed | tf_op | source)
XLA Modules:
  0.0 138.6 jit_solution(12249572886943174631)
XLA Ops:
  0.6 132.9 %shard_map.85 = (bf16[1,32,8,512]{3,2,1,0:T(8,128)(2,1)}, bf16[1,32,8,512]{3,2,1,0:T(8,128)(2,1)}, f32[1,1]{1,0:T(1,128)}) custom-call(bf16[1,32,8,512]{3,2,1,0:T(8,128)(2,1)} %psi_hbm.1, bf16[1,32,8,512]{3,2,1,0:T(8,128)(2,1)} %pc_hbm.1, bf16[3,1,512,512]{3,2,1,0:T(8,128)(2,1)} %left_hbm.1, bf16[3,1,512,512]{3,2,1,0:T(8,128)(2,1)} %right_hbm.1, ...), custom_call_target="tpu_custom_call" | custom-call | flops 2200000000 | bytes 2000000 | tf_op jit(solution)/shard_map/pallas_call | solution.py:740
  133.6 1.7 %copy.12 = bf16[1,32,8,512]{3,2,1,0:T(8,128)(2,1)} copy(bf16[1,32,8,512]{3,2,1,0:T(8,128)(2,1)} %get-tuple-element.12) | data formatting | bytes 524288
  135.2 1.7 %copy.13 = bf16[1,32,8,512]{3,2,1,0:T(8,128)(2,1)} copy(bf16[1,32,8,512]{3,2,1,0:T(8,128)(2,1)} %get-tuple-element.13) | data formatting | bytes 524288

commit v5 on v4

--- a/solution.py
+++ b/solution.py
@@ -30,6 +30,18 @@
 
 def iota(shape, axis):
     return lax.broadcasted_iota(jnp.int32, shape, axis)
+
+
+def wrap(value, size):
+    return jnp.where(value >= size, value - size, value)
+
+
+def over(value, bits):
+    return lax.shift_right_logical(value, jnp.full_like(value, bits))
+
+
+def under(value, bits):
+    return value - lax.shift_left(over(value, bits), jnp.full_like(value, bits))
 
 
 def partial_sum(x):
@@ -69,6 +81,7 @@
     land_env,
     env,
     kron,
+    swap,
     to_new,
     to_old,
     start_rows,
@@ -111,10 +124,13 @@
 ):
     z = lax.axis_index("tr")
     sec = lax.axis_index("sec")
-    k = sec // 2
-    core = lax.rem(sec, 2)
-    y = k // 4
-    x = lax.rem(k, 4)
+    k = over(sec, 1)
+    core = sec - 2 * k
+    y = over(k, 2)
+    x = k - 4 * y
+    next_z = wrap(z + 1, TR)
+    rows_at = [y] + [wrap(y + d, 4) for d in range(1, 4)]
+    columns_at = [x] + [wrap(x + d, 4) for d in range(1, 4)]
 
     def ring(z2):
         return {"tr": z2}
@@ -127,16 +143,13 @@
 
     def ring_peer(i):
         m = turned(i + k)
-        step = m // 2 + 1
-        return lax.rem(z + jnp.where(lax.rem(m, 2) == 0, step, TR - step), TR)
-
-    def ring_source(i):
-        m = turned(i + k)
-        step = m // 2 + 1
-        return lax.rem(z + jnp.where(lax.rem(m, 2) == 0, TR - step, step), TR)
+        half = over(m, 1)
+        step = half + 1
+        return wrap(z + jnp.where(m == 2 * half, step, TR - step), TR)
 
     def plane_peer(i):
-        return 4 * lax.rem(y + i // 4, 4) + lax.rem(x + lax.rem(i, 4), 4)
+        down = over(i, 2)
+        return 4 * wrap(y + down, 4) + wrap(x + i - 4 * down, 4)
 
     def remote(src, dst, send_sem, recv_sem, device):
         return pltpu.make_async_remote_copy(
@@ -150,7 +163,7 @@
 
     def several(ref, count, send_sem, recv_sem):
         part = ref.at[pl.ds(0, count)]
-        return remote(part, part, send_sem, recv_sem, ring(lax.rem(z + 1, TR)))
+        return remote(part, part, send_sem, recv_sem, ring(next_z))
 
     ends = []
 
@@ -176,12 +189,12 @@
     barrier = pltpu.get_barrier_semaphore()
 
     def greet_tr(i, carry):
-        pl.semaphore_signal(barrier, inc=1, device_id=ring(lax.rem(z + i, TR)), device_id_type=MESH)
+        pl.semaphore_signal(barrier, inc=1, device_id=ring(wrap(z + i, TR)), device_id_type=MESH)
         return carry
 
     def greet_sec(i, carry):
         pl.semaphore_signal(
-            barrier, inc=1, device_id={"sec": lax.rem(sec + i, SEC)}, device_id_type=MESH
+            barrier, inc=1, device_id={"sec": wrap(sec + i, SEC)}, device_id_type=MESH
         )
         return carry
 
@@ -211,22 +224,20 @@
     line = iota((LINES, LINES), 0)
     other = iota((LINES, LINES), 1)
 
+    for n, (one, two) in enumerate(((line, other), (other, line))):
+        same = one == under(two, 3) * ROWS + over(two, 3)
+        swap[n] = same.astype(BF16)
+
     def to_phys_major(value):
-        matrix = ((line // ROWS) == lax.rem(other, PHYS)) & (
-            lax.rem(line, ROWS) == (other // PHYS)
-        )
-        return dot(matrix.astype(BF16), value)
+        return dot(swap[0], value)
 
     def to_row_major(value):
-        matrix = ((other // ROWS) == lax.rem(line, PHYS)) & (
-            lax.rem(other, ROWS) == (line // PHYS)
-        )
-        return dot(matrix.astype(BF16), value)
+        return dot(swap[1], value)
 
     loads[3].wait()
     used_left = sizes[0, 0]
     used_right = sizes[0, 1]
-    keep = ((z * ROWS + iota((LINES, WIDTH), 0) // PHYS) < used_right) & (
+    keep = ((z * ROWS + over(iota((LINES, WIDTH), 0), 3)) < used_right) & (
         iota((LINES, WIDTH), 1) < used_left
     )
     loads[0].wait()
@@ -260,7 +271,7 @@
             middle.at[index],
             move_send_sem.at[n, 0],
             move_one_sem.at[n, index],
-            ring(lax.rem(z + 1, TR)),
+            ring(next_z),
         )
 
     def move_in_ring(n, middle, target):
@@ -331,13 +342,13 @@
         return env[m, c].reshape(WIDTH, WIDTH)
 
     def piece(m, dy, dx, part=(pl.ds(0, ROWS), pl.ds(0, WIDTH))):
-        return env.at[m, :, lax.rem(y + dy + 4, 4), lax.rem(x + dx + 4, 4), part[0], part[1]]
+        return env.at[m, :, rows_at[dy % 4], columns_at[dx % 4], part[0], part[1]]
 
     def row_set(m, dy, part):
-        return env.at[m, :, lax.rem(y + dy + 4, 4), :, part[0], part[1]]
+        return env.at[m, :, rows_at[dy % 4], :, part[0], part[1]]
 
     def column_set(m, dx, part):
-        return env.at[m, :, :, lax.rem(x + dx + 4, 4), part[0], part[1]]
+        return env.at[m, :, :, columns_at[dx % 4], part[0], part[1]]
 
     def scatter_copy(m, d, n):
         return remote(
@@ -398,7 +409,7 @@
                 land_env.at[m],
                 own_send_sem.at[m],
                 scatter_recv_sem.at[m],
-                ring(lax.rem(z + 1, TR)),
+                ring(next_z),
             ).wait_recv()
 
         @pl.when(shift != 0)
@@ -423,7 +434,7 @@
     quarters = [(pl.ds(n // 2 * 16, 16), pl.ds(n % 2 * HALF, HALF)) for n in range(4)]
 
     def hop(m, n, ref, dy, dx):
-        target = 4 * lax.rem(y + dy + 4, 4) + lax.rem(x + dx + 4, 4)
+        target = 4 * rows_at[dy % 4] + columns_at[dx % 4]
         return remote(ref, ref, gather_send_sem.at[m], gather_recv_sem.at[m, n], plane(target))
 
     def gather_one(m):
@@ -472,7 +483,7 @@
     def gather_end(m):
         sent = own_env.at[m, :, pl.ds(0, WIDTH - ROWS), :]
         remote(
-            sent, sent, gather_send_sem.at[m], own_recv_sem.at[m], ring(lax.rem(z + 1, TR))
+            sent, sent, gather_send_sem.at[m], own_recv_sem.at[m], ring(next_z)
         ).wait_send()
 
     def turn(n, sources, targets, begin, count):
@@ -495,7 +506,7 @@
             targets[place, k] = sources[place, k]
         part = target.at[:, pl.ds(0, TR - 1)]
         done = remote(
-            part, part, turn_send_sem.at[n], turn_recv_sem.at[n], ring(lax.rem(z + 1, TR))
+            part, part, turn_send_sem.at[n], turn_recv_sem.at[n], ring(next_z)
         )
         ends.append(done)
         return done
@@ -533,14 +544,15 @@
     wide_other = iota((WIDTH, WIDTH), 1)
 
     def old_row(r):
-        return lax.rem(r, 32) // 2 * 32 + r // 32 * 2 + lax.rem(r, 2)
+        pair = over(r, 1)
+        return under(pair, 4) * 32 + over(r, 5) * 2 + r - 2 * pair
 
     to_new[...] = (old_row(wide_line) == wide_other).astype(BF16)
     gather_two(0)
     to_old[...] = (old_row(wide_other) == wide_line).astype(BF16)
     loads[2].wait()
-    spread = ((iota((LINES, PHYS), 0) // ROWS) == iota((LINES, PHYS), 1)).astype(BF16)
-    same_row = lax.rem(line, ROWS) == lax.rem(other, ROWS)
+    spread = (over(iota((LINES, PHYS), 0), 5) == iota((LINES, PHYS), 1)).astype(BF16)
+    same_row = under(line, 5) == under(other, 5)
     for c in range(3):
         mixed = dot_nt(dot(spread, mix[c]).astype(BF16), spread)
         kron[c] = jnp.where(same_row, mixed, 0.0).astype(BF16)
@@ -617,7 +629,7 @@
                 red_sec.at[h, sec],
                 red_send_sem.at[h, 1],
                 red_recv_sem.at[h, 1],
-                {"sec": lax.rem(sec + i, SEC)},
+                {"sec": wrap(sec + i, SEC)},
             ).start()
             return carry
 
@@ -755,6 +767,7 @@
             pltpu.VMEM((2, 3, ROWS, WIDTH), BF16),
             pltpu.VMEM((2, 3, 4, 4, ROWS, WIDTH), BF16),
             pltpu.VMEM((3, LINES, LINES), BF16),
+            pltpu.VMEM((2, LINES, LINES), BF16),
             pltpu.VMEM((WIDTH, WIDTH), BF16),
             pltpu.VMEM((WIDTH, WIDTH), BF16),
             pltpu.VMEM((LINES, WIDTH), BF16),

time: 139 us -> 139 us (level)
  no operation moved by 1% of the time
where the time goes in v5:
time: 139 us
  Pallas kernels  133 us (96%)
  local copies, waits for them, and re-layouts  3.34 us (2%)
  between operations  2.34 us (2%)
    pallas_call x1, Pallas kernels, body(): pl.pallas_call(kernel, out_shape=(jax.ShapeDtypeStruct(psi.shape, BF16),...  133 us
    unnamed x2, local copies, waits for them, and re-layouts  3.34 us

profile of v5, /device:TPU:1, one launch (start us, length us, event | category | flops | bytes accessed | tf_op | source)
XLA Modules:
  0.0 138.6 jit_solution(2450940952697477515)
XLA Ops:
  0.6 132.9 %shard_map.85 = (bf16[1,32,8,512]{3,2,1,0:T(8,128)(2,1)}, bf16[1,32,8,512]{3,2,1,0:T(8,128)(2,1)}, f32[1,1]{1,0:T(1,128)}) custom-call(bf16[1,32,8,512]{3,2,1,0:T(8,128)(2,1)} %psi_hbm.1, bf16[1,32,8,512]{3,2,1,0:T(8,128)(2,1)} %pc_hbm.1, bf16[3,1,512,512]{3,2,1,0:T(8,128)(2,1)} %left_hbm.1, bf16[3,1,512,512]{3,2,1,0:T(8,128)(2,1)} %right_hbm.1, ...), custom_call_target="tpu_custom_call" | custom-call | flops 2200000000 | bytes 2000000 | tf_op jit(solution)/shard_map/pallas_call | solution.py:752
  133.6 1.7 %copy.12 = bf16[1,32,8,512]{3,2,1,0:T(8,128)(2,1)} copy(bf16[1,32,8,512]{3,2,1,0:T(8,128)(2,1)} %get-tuple-element.12) | data formatting | bytes 524288
  135.2 1.7 %copy.13 = bf16[1,32,8,512]{3,2,1,0:T(8,128)(2,1)} copy(bf16[1,32,8,512]{3,2,1,0:T(8,128)(2,1)} %get-tuple-element.13) | data formatting | bytes 524288

commit v6 on v5

--- a/solution.py
+++ b/solution.py
@@ -84,6 +84,8 @@
     swap,
     to_new,
     to_old,
+    right_old,
+    left_turned,
     start_rows,
     cols_send,
     cols_mid,
@@ -585,6 +587,8 @@
     gather_three(1)
     pc_done = move_in_ring(1, pc_mid, pc_new)
     gather_four(1)
+    for c in range(3):
+        right_old[c] = dot(env_matrix(0, c), to_old[...]).astype(BF16)
     gather_wait(1)
     total = None
     for c in range(3):
@@ -649,6 +653,8 @@
     tr_start(0, block).wait_recv()
     sums_done = sec_start(0, jnp.sum(red_tr[0], axis=0))
     back(2, first_send, first_old, 0, 5)
+    for c in range(3):
+        left_turned[c] = env_matrix(1, c).T
     sums_done.wait_recv()
     ss, sw, spw, sps = means(jnp.sum(red_sec[0], axis=0))
     norm = lax.rsqrt(ss + EPSILON)
@@ -667,7 +673,7 @@
 
     def left_part(c, value):
         mixed = dot(kron[c], value).astype(BF16)
-        return dot_nt(mixed, env_matrix(1, c)).astype(BF16)
+        return dot(mixed, left_turned[c]).astype(BF16)
 
     store_columns(half_send.at[0], left_part(0, trial_bf))
     turns = [turn(3, half_send, half_recv, 0, 1)]
@@ -686,8 +692,7 @@
     for c in range(3):
         if c < 2:
             turns[c].wait_recv()
-        half = dot(to_old[...], half_recv[c].reshape(WIDTH, HALF)).astype(BF16)
-        term = dot(env_matrix(0, c), half)
+        term = dot(right_old[c], half_recv[c].reshape(WIDTH, HALF))
         total = term if total is None else total + term
     second_send[...] = total.astype(BF16).reshape(TR, ROWS, HALF)
     back(3, second_send, second_old, 0, TR - 1)
@@ -770,6 +775,8 @@
             pltpu.VMEM((2, LINES, LINES), BF16),
             pltpu.VMEM((WIDTH, WIDTH), BF16),
             pltpu.VMEM((WIDTH, WIDTH), BF16),
+            pltpu.VMEM((3, WIDTH, WIDTH), BF16),
+            pltpu.VMEM((3, WIDTH, WIDTH), BF16),
             pltpu.VMEM((LINES, WIDTH), BF16),
             pltpu.VMEM(columns, BF16),
             pltpu.VMEM(columns, BF16),

time: 139 us -> 139 us (level)
  no operation moved by 1% of the time
where the time goes in v6:
time: 139 us
  Pallas kernels  133 us (96%)
  local copies, waits for them, and re-layouts  3.34 us (2%)
  between operations  2.34 us (2%)
    pallas_call x1, Pallas kernels, body(): pl.pallas_call(kernel, out_shape=(jax.ShapeDtypeStruct(psi.shape, BF16),...  133 us
    unnamed x2, local copies, waits for them, and re-layouts  3.34 us

profile of v6, /device:TPU:1, one launch (start us, length us, event | category | flops | bytes accessed | tf_op | source)
XLA Modules:
  0.0 138.7 jit_solution(18245682580374226074)
XLA Ops:
  0.6 133.0 %shard_map.85 = (bf16[1,32,8,512]{3,2,1,0:T(8,128)(2,1)}, bf16[1,32,8,512]{3,2,1,0:T(8,128)(2,1)}, f32[1,1]{1,0:T(1,128)}) custom-call(bf16[1,32,8,512]{3,2,1,0:T(8,128)(2,1)} %psi_hbm.1, bf16[1,32,8,512]{3,2,1,0:T(8,128)(2,1)} %pc_hbm.1, bf16[3,1,512,512]{3,2,1,0:T(8,128)(2,1)} %left_hbm.1, bf16[3,1,512,512]{3,2,1,0:T(8,128)(2,1)} %right_hbm.1, ...), custom_call_target="tpu_custom_call" | custom-call | flops 2200000000 | bytes 2000000 | tf_op jit(solution)/shard_map/pallas_call | solution.py:757
  133.6 1.7 %copy.12 = bf16[1,32,8,512]{3,2,1,0:T(8,128)(2,1)} copy(bf16[1,32,8,512]{3,2,1,0:T(8,128)(2,1)} %get-tuple-element.12) | data formatting | bytes 524288
  135.3 1.7 %copy.13 = bf16[1,32,8,512]{3,2,1,0:T(8,128)(2,1)} copy(bf16[1,32,8,512]{3,2,1,0:T(8,128)(2,1)} %get-tuple-element.13) | data formatting | bytes 524288

commit v7 on v6

--- a/solution.py
+++ b/solution.py
@@ -101,8 +101,10 @@
     half_send,
     half_recv,
     first_send,
+    first_mid,
     first_old,
     second_send,
+    second_mid,
     second_old,
     red_send,
     red_tr,
@@ -149,6 +151,12 @@
         step = half + 1
         return wrap(z + jnp.where(m == 2 * half, step, TR - step), TR)
 
+    def ring_source(i):
+        m = turned(i + k)
+        half = over(m, 1)
+        step = half + 1
+        return wrap(z + jnp.where(m == 2 * half, TR - step, step), TR)
+
     def plane_peer(i):
         down = over(i, 2)
         return 4 * wrap(y + down, 4) + wrap(x + i - 4 * down, 4)
@@ -207,21 +215,8 @@
         device_id={"tr": lax.rem(z + 2 * core - 1 + TR, TR), "sec": partner},
         device_id_type=MESH,
     )
-    def greet_far(j, carry):
-        @pl.when((k != z) | (j != k))
-        def _():
-            pl.semaphore_signal(
-                barrier,
-                inc=1,
-                device_id={"tr": k, "sec": 2 * j + core},
-                device_id_type=MESH,
-            )
-
-        return carry
-
     lax.fori_loop(1, SEC, greet_sec, 0)
     lax.fori_loop(1, TR, greet_tr, 0)
-    lax.fori_loop(0, TR, greet_far, 0)
 
     line = iota((LINES, LINES), 0)
     other = iota((LINES, LINES), 1)
@@ -249,7 +244,7 @@
     loads[1].wait()
     pc_send[...] = pc_in[...].astype(F32).reshape(TR, 2 * PHYS, WIDTH).astype(BF16)
 
-    pl.semaphore_wait(barrier, TR + SEC - 1 + TR - jnp.where(k == z, 1, 0))
+    pl.semaphore_wait(barrier, TR + SEC - 1)
 
     def move_in_plane(n, source, middle):
         def send(i, carry):
@@ -300,45 +295,46 @@
         ends.append(done)
         return done
 
-    def back(n, source, target, begin, end):
+    def back_in_ring(n, source, middle):
         def send(i, carry):
             peer = ring_peer(i)
             remote(
                 source.at[peer],
-                target.at[k],
+                middle.at[z],
                 move_send_sem.at[n, 0],
-                move_two_sem.at[n],
-                {"tr": peer, "sec": 2 * z + core},
+                move_one_sem.at[n, z],
+                ring(peer),
             ).start()
             return carry
 
-        lax.fori_loop(begin, end, send, 0)
-
-    def back_home(n, source, target):
-        @pl.when(z != k)
-        def _():
-            remote(
-                source.at[z],
-                target.at[k],
-                move_send_sem.at[n, 0],
-                move_two_sem.at[n],
-                {"tr": z, "sec": 2 * z + core},
-            ).start()
-
-        @pl.when(z == k)
-        def _():
-            target[k] = source[k]
-
-    def back_wait(n, target, sent):
-        for same in range(2):
-
-            @pl.when((z == k) if same else (z != k))
+        lax.fori_loop(0, TR - 1, send, 0)
+        middle[z] = source[z]
+        ends.append(several(middle, TR - 1, move_send_sem.at[n, 0], move_two_sem.at[n]))
+
+    def back_in_plane(n, middle, target):
+        def forward(index):
+            @pl.when(index != k)
             def _():
-                done = several(target, TR - same, move_send_sem.at[n, 0], move_two_sem.at[n])
-                if sent:
-                    done.wait_send()
-                else:
-                    done.wait_recv()
+                remote(
+                    middle.at[index],
+                    target.at[k],
+                    move_send_sem.at[n, 1],
+                    move_two_sem.at[n],
+                    plane(index),
+                ).start()
+
+        def send(i, carry):
+            index = ring_source(i)
+            arrived(n, middle, index).wait_recv()
+            forward(index)
+            return carry
+
+        forward(z)
+        lax.fori_loop(0, TR - 1, send, 0)
+        target[k] = middle[k]
+        done = several(target, TR - 1, move_send_sem.at[n, 1], move_two_sem.at[n])
+        ends.append(done)
+        return done
 
     def env_matrix(m, c):
         return env[m, c].reshape(WIDTH, WIDTH)
@@ -652,7 +648,7 @@
     block = jnp.concatenate([partial_sum(part) for part in parts] * 2, axis=0)
     tr_start(0, block).wait_recv()
     sums_done = sec_start(0, jnp.sum(red_tr[0], axis=0))
-    back(2, first_send, first_old, 0, 5)
+    back_in_ring(2, first_send, first_mid)
     for c in range(3):
         left_turned[c] = env_matrix(1, c).T
     sums_done.wait_recv()
@@ -683,8 +679,6 @@
         store_columns(half_send.at[way + 1], left_part(way + 1, inside(way, near_vec[way])))
     turns.append(turn(4, half_send, half_recv, 1, 2))
     trial_turn = turn(5, half_send, half_recv, 3, 1)
-    back(2, first_send, first_old, 5, TR - 1)
-    back_home(2, first_send, first_old)
     second = trial_bf.astype(F32)
     tt = partial_sum(trial * trial)
     t0 = partial_sum(second * image0)
@@ -695,8 +689,7 @@
         term = dot(right_old[c], half_recv[c].reshape(WIDTH, HALF))
         total = term if total is None else total + term
     second_send[...] = total.astype(BF16).reshape(TR, ROWS, HALF)
-    back(3, second_send, second_old, 0, TR - 1)
-    back_home(3, second_send, second_old)
+    back_in_ring(3, second_send, second_mid)
     image1_cols = total.astype(BF16).astype(F32)
     trial_turn.wait_recv()
     trial_cols = dot(to_old[...], half_recv[3].reshape(WIDTH, HALF))
@@ -705,6 +698,8 @@
     block = jnp.concatenate([tt, s1, t0, t1] * 2, axis=0)
     sec_start(1, block).wait_recv()
     sums_done = tr_start(1, jnp.sum(red_sec[1], axis=0))
+    first_done = back_in_plane(2, first_mid, first_old)
+    second_done = back_in_plane(3, second_mid, second_old)
     sums_done.wait_recv()
     tt, s1, t0, t1 = means(jnp.sum(red_tr[1], axis=0))
 
@@ -721,7 +716,7 @@
     two = weight_two * scale * grow
     energy_out[...] = energy
 
-    back_wait(2, first_old, False)
+    first_done.wait_recv()
     old_image = first_old[...].reshape(LINES, WIDTH).astype(F32)
     old_start = start_rows[...].astype(F32)
     old_factors = pc_send[...].reshape(LINES, WIDTH).astype(F32)
@@ -729,7 +724,7 @@
     ritz = one * old_start + two * old_trial
     psi_out[...] = ritz.reshape(ROWS, PHYS, WIDTH).astype(BF16)[None]
     partial = one * old_image - energy * ritz
-    back_wait(3, second_old, False)
+    second_done.wait_recv()
     residual = partial + two * to_row_major(phys_major(second_old[...]))
     res_out[...] = residual.reshape(ROWS, PHYS, WIDTH).astype(BF16)[None]
 
@@ -741,8 +736,6 @@
         def _():
             hand_over(m).wait_send()
 
-    back_wait(2, first_old, True)
-    back_wait(3, second_old, True)
     for end in ends:
         end.wait_send()
 
@@ -793,6 +786,8 @@
             pltpu.VMEM(fours, BF16),
             pltpu.VMEM(rows, BF16),
             pltpu.VMEM(rows, BF16),
+            pltpu.VMEM(rows, BF16),
+            pltpu.VMEM(columns, BF16),
             pltpu.VMEM(columns, BF16),
             pltpu.VMEM(columns, BF16),
             pltpu.VMEM((2, 2, 8, 128), F32),

time: 139 us -> 138 us (level); the launches traced: 139 us -> 136 us
  Pallas kernels: 133 us -> 130 us
    pallas_call x1, Pallas kernels: 133 us -> 130 us  [body(): pl.pallas_call(kernel, out_shape=(jax.ShapeDtypeStruct(psi.shape, BF16),...]
where the time goes in v7:
time: 138 us; the launch traced here: 136 us
  Pallas kernels  130 us (94%)
  local copies, waits for them, and re-layouts  3.34 us (2%)
  between operations  2.34 us (2%)
    pallas_call x1, Pallas kernels, body(): pl.pallas_call(kernel, out_shape=(jax.ShapeDtypeStruct(psi.shape, BF16),...  130 us
    unnamed x2, local copies, waits for them, and re-layouts  3.34 us

profile of v7, /device:TPU:1, one launch (start us, length us, event | category | flops | bytes accessed | tf_op | source)
XLA Modules:
  0.0 136.0 jit_solution(2267108904714504179)
XLA Ops:
  0.6 130.4 %shard_map.85 = (bf16[1,32,8,512]{3,2,1,0:T(8,128)(2,1)}, bf16[1,32,8,512]{3,2,1,0:T(8,128)(2,1)}, f32[1,1]{1,0:T(1,128)}) custom-call(bf16[1,32,8,512]{3,2,1,0:T(8,128)(2,1)} %psi_hbm.1, bf16[1,32,8,512]{3,2,1,0:T(8,128)(2,1)} %pc_hbm.1, bf16[3,1,512,512]{3,2,1,0:T(8,128)(2,1)} %left_hbm.1, bf16[3,1,512,512]{3,2,1,0:T(8,128)(2,1)} %right_hbm.1, ...), custom_call_target="tpu_custom_call" | custom-call | flops 2200000000 | bytes 2000000 | tf_op jit(solution)/shard_map/pallas_call | solution.py:750
  131.0 1.7 %copy.12 = bf16[1,32,8,512]{3,2,1,0:T(8,128)(2,1)} copy(bf16[1,32,8,512]{3,2,1,0:T(8,128)(2,1)} %get-tuple-element.12) | data formatting | bytes 524288
  132.7 1.7 %copy.13 = bf16[1,32,8,512]{3,2,1,0:T(8,128)(2,1)} copy(bf16[1,32,8,512]{3,2,1,0:T(8,128)(2,1)} %get-tuple-element.13) | data formatting | bytes 524288
